TPU v7x, 256 devices: a whole 4x4x8 slice. The times are simulated.
256 devices in a mesh: dp: 16 (over x, y), tensor: 16 (over z, core).
Axes of the slice: x: 4, y: 4, z: 8, core: 2. Of those that a mesh axis runs over, the one named last changes fastest.
Arguments:
- tokens: bfloat16 [6144, 18432], P('dp', 'tensor'), may hold values from -6 to 6
- target: bfloat16 [6144, 18432], P('dp', 'tensor'), may hold values from -6 to 6
- first_in: float32 [512, 18432], P('dp', 'tensor'), may hold values from -0.046875 to 0.046875
- first_out: float32 [512, 36864], P('dp', 'tensor'), may hold values from -0.25 to 0.25
- second_in: float32 [512, 36864], P('dp', 'tensor'), may hold values from -0.03125 to 0.03125
- second_out: float32 [512, 18432], P('dp', 'tensor'), may hold values from -0.25 to 0.25
- width_mean: float32 [2, 512, 18432], P(None, 'dp', 'tensor'), may hold values from -0.00030517578 to 0.00030517578
- width_square: float32 [2, 512, 18432], P(None, 'dp', 'tensor'), may hold values from 1.7660635e-10 to 1.7660636e-08
- hidden_mean: float32 [2, 512, 36864], P(None, 'dp', 'tensor'), may hold values from -0.00030517578 to 0.00030517578
- hidden_square: float32 [2, 512, 36864], P(None, 'dp', 'tensor'), may hold values from 1.7660635e-10 to 1.7660636e-08
Outputs:
- new_first_in: float32 [512, 18432], P('dp', 'tensor')
- new_first_out: float32 [512, 36864], P('dp', 'tensor')
- new_second_in: float32 [512, 36864], P('dp', 'tensor')
- new_second_out: float32 [512, 18432], P('dp', 'tensor')
- new_width_mean: float32 [2, 512, 18432], P(None, 'dp', 'tensor')
- new_width_square: float32 [2, 512, 18432], P(None, 'dp', 'tensor')
- new_hidden_mean: float32 [2, 512, 36864], P(None, 'dp', 'tensor')
- new_hidden_square: float32 [2, 512, 36864], P(None, 'dp', 'tensor')
- loss_value: float32 [], replicated
All inputs are finite; a program needn't handle non-finite values.
Results may differ from a plain program's by a relative error of at most 0.0059.
Values may be sent and summed in bfloat16 or wider, within the bound.
A program may use at most 128 MiB of HBM per device.

v0:
```python
import jax
import jax.numpy as jnp
from jax import lax
from jax.sharding import PartitionSpec as P

beta_one = 0.9
beta_two = 0.95
learn_rate = 0.1
tiny_eps = 1e-08


def adam_update(param, grad, mean, square):
    new_mean = beta_one * mean + (1.0 - beta_one) * grad
    new_square = beta_two * square + (1.0 - beta_two) * grad * grad
    corrected = new_mean / (1.0 - beta_one**10)
    spread = jnp.sqrt(new_square / (1.0 - beta_two**10)) + tiny_eps
    return (param - learn_rate * corrected / spread, new_mean, new_square)


def last_dims(left, right):
    return lax.dot_general(
        left, right, (((1,), (1,)), ((), ())), preferred_element_type=jnp.float32
    )


def first_dims(left, right):
    return lax.dot_general(
        left, right, (((0,), (0,)), ((), ())), preferred_element_type=jnp.float32
    )


def shards(
    tokens,
    target,
    first_in,
    first_out,
    second_in,
    second_out,
    width_mean,
    width_square,
    hidden_mean,
    hidden_square,
):
    copies = (
        first_in.astype(jnp.bfloat16),
        first_out.astype(jnp.bfloat16),
        second_in.astype(jnp.bfloat16),
        second_out.astype(jnp.bfloat16),
    )
    copy_pi, copy_po, copy_qi, copy_qo = (
        lax.all_gather(copies[0], "dp", axis=0, tiled=True),
        lax.all_gather(copies[1], "dp", axis=0, tiled=True),
        lax.all_gather(copies[2], "dp", axis=0, tiled=True),
        lax.all_gather(copies[3], "dp", axis=0, tiled=True),
    )
    total_tokens = tokens.shape[0] * lax.axis_size("dp")
    rank_in = lax.psum(last_dims(tokens, copy_pi), "tensor").astype(jnp.bfloat16)
    pre = jnp.dot(rank_in, copy_po, preferred_element_type=jnp.float32)
    hidden = jnp.square(jnp.maximum(pre, 0.0)).astype(jnp.bfloat16)
    rank_out = lax.psum(last_dims(hidden, copy_qi), "tensor").astype(jnp.bfloat16)
    misfit = jnp.dot(rank_out, copy_qo, preferred_element_type=jnp.float32) - target.astype(
        jnp.float32
    )
    local_loss = jnp.sum(misfit * misfit)
    loss_total = lax.psum(local_loss, ("dp", "tensor"))
    grad_out = (misfit / total_tokens).astype(jnp.bfloat16)
    copy_pi, copy_po, copy_qi, copy_qo = (
        lax.all_gather(copies[0], "dp", axis=0, tiled=True),
        lax.all_gather(copies[1], "dp", axis=0, tiled=True),
        lax.all_gather(copies[2], "dp", axis=0, tiled=True),
        lax.all_gather(copies[3], "dp", axis=0, tiled=True),
    )
    grad_rank_out = lax.psum(last_dims(grad_out, copy_qo), "tensor").astype(jnp.bfloat16)
    grad_pre = (
        jnp.dot(grad_rank_out, copy_qi, preferred_element_type=jnp.float32)
        * 2.0
        * jnp.maximum(pre, 0.0)
    ).astype(jnp.bfloat16)
    hidden_cols = hidden.shape[1]
    hidden_rows = lax.psum_scatter(
        jnp.concatenate([first_dims(rank_in, grad_pre), first_dims(grad_rank_out, hidden)], axis=1),
        "dp",
        scatter_dimension=0,
        tiled=True,
    )
    grad_po = hidden_rows[:, :hidden_cols]
    grad_qi = hidden_rows[:, hidden_cols:]
    grad_rank_in = lax.psum(last_dims(grad_pre, copy_po), "tensor").astype(jnp.bfloat16)
    width_cols = tokens.shape[1]
    width_rows = lax.psum_scatter(
        jnp.concatenate([first_dims(grad_rank_in, tokens), first_dims(rank_out, grad_out)], axis=1),
        "dp",
        scatter_dimension=0,
        tiled=True,
    )
    grad_pi = width_rows[:, :width_cols]
    grad_qo = width_rows[:, width_cols:]
    local_squares = (
        jnp.sum(grad_pi * grad_pi)
        + jnp.sum(grad_po * grad_po)
        + jnp.sum(grad_qi * grad_qi)
        + jnp.sum(grad_qo * grad_qo)
    )
    squares = lax.psum(local_squares, ("dp", "tensor"))
    scale = 1.0 / jnp.maximum(jnp.sqrt(squares), 1.0)
    new_pi, mean_pi, square_pi = adam_update(
        first_in, grad_pi * scale, width_mean[0], width_square[0]
    )
    new_qo, mean_qo, square_qo = adam_update(
        second_out, grad_qo * scale, width_mean[1], width_square[1]
    )
    new_po, mean_po, square_po = adam_update(
        first_out, grad_po * scale, hidden_mean[0], hidden_square[0]
    )
    new_qi, mean_qi, square_qi = adam_update(
        second_in, grad_qi * scale, hidden_mean[1], hidden_square[1]
    )
    loss_value = loss_total / (2.0 * total_tokens)
    return (
        new_pi,
        new_po,
        new_qi,
        new_qo,
        jnp.stack([mean_pi, mean_qo]),
        jnp.stack([square_pi, square_qo]),
        jnp.stack([mean_po, mean_qi]),
        jnp.stack([square_po, square_qi]),
        loss_value,
    )


def solution(mesh):
    placed = (
        P("dp", "tensor"),
        P("dp", "tensor"),
        P("dp", "tensor"),
        P("dp", "tensor"),
        P("dp", "tensor"),
        P("dp", "tensor"),
        P(None, "dp", "tensor"),
        P(None, "dp", "tensor"),
        P(None, "dp", "tensor"),
        P(None, "dp", "tensor"),
    )
    return jax.shard_map(
        shards,
        mesh=mesh,
        in_specs=placed,
        out_specs=(
            P("dp", "tensor"),
            P("dp", "tensor"),
            P("dp", "tensor"),
            P("dp", "tensor"),
            P(None, "dp", "tensor"),
            P(None, "dp", "tensor"),
            P(None, "dp", "tensor"),
            P(None, "dp", "tensor"),
            P(),
        ),
        check_vma=False,
    )
```

profile of v0, /device:TPU:1, one launch (start us, length us, event | category | flops | bytes accessed | tf_op | source)
XLA Modules:
  0.0 625.8 jit_solution(9789129249690012647)
XLA Ops:
  7.2 0.0 copy-start
  7.2 0.0 all-gather.5.cloned.1.call-start
  7.2 1.6 convert_element_type.36
  8.9 0.0 all-gather.5.cloned.1.call-update
  8.9 0.0 all-gather.7.cloned.1.call-start
  8.9 1.6 convert_element_type.38
  10.6 0.0 all-gather.7.cloned.1.call-update
  10.6 0.0 all-gather.9.cloned.1.call-start
  10.6 1.6 convert_element_type.40
  12.3 0.0 all-gather.9.cloned.1.call-update
  12.3 0.0 all-gather.11.cloned.1.call-start
  12.4 1.6 convert_element_type.42
  13.9 0.0 all-gather.11.cloned.1.call-update
  13.9 0.0 reduce-scatter.3.cloned.1.call-start
  14.0 48.2 %all-gather.5.cloned.1.call-done = bf16[512,1152]{1,0:T(8,128)(2,1)} async-done(((bf16[32,1152]{1,0:T(8,128)(2,1)}), bf16[512,1152]{1,0:T(8,128)(2,1)}) %all-gather.5.cloned.1.call-update) | async-done | bytes 1179664 | tf_op jit(solution)/shard_map/all_gather | solution.py:51
  62.2 0.0 copy-done
  62.2 2.0 fusion.29
  64.1 54.6 %all-reduce.5 = bf16[384,512]{1,0:T(8,128)(2,1)S(1)} all-reduce(f32[384,512]{1,0:T(8,128)S(1)} %fusion.29), channel_id=1, replica_groups=mesh['dp'=16,'tensor'=16] {'tensor'}, use_global_device_ids=true, to_apply=%region_0.0 | all-reduce | flops 196608 | bytes 1179648 | tf_op jit(solution)/shard_map/psum | solution.py:57
  118.7 0.0 all-gather.7.cloned.1.call-done
  118.8 4.5 convolution_maximum_fusion
  123.3 45.3 %all-gather.9.cloned.1.call-done = bf16[512,2304]{1,0:T(8,128)(2,1)} async-done(((bf16[32,2304]{1,0:T(8,128)(2,1)}), bf16[512,2304]{1,0:T(8,128)(2,1)}) %all-gather.9.cloned.1.call-update) | async-done | bytes 2359312 | tf_op jit(solution)/shard_map/all_gather | solution.py:53
  168.5 3.8 fusion.3
  172.4 54.2 %all-reduce.6 = bf16[384,512]{1,0:T(8,128)(2,1)S(1)} all-reduce(f32[384,512]{1,0:T(8,128)S(1)} %fusion.3), channel_id=1, replica_groups=mesh['dp'=16,'tensor'=16] {'tensor'}, use_global_device_ids=true, to_apply=%region_1.0 | all-reduce | flops 196608 | bytes 1179648 | tf_op jit(solution)/shard_map/psum | solution.py:60
  226.5 0.0 all-gather.11.cloned.1.call-done
  226.6 0.0 copy-done.8
  226.6 2.6 multiply_reduce_fusion
  229.2 2.3 fusion.6
  231.5 0.0 copy-done.3
  231.5 0.7 fusion.7
  232.3 53.8 %all-reduce.7 = bf16[384,512]{1,0:T(8,128)(2,1)S(1)} all-reduce(f32[384,512]{1,0:T(8,128)S(1)} %fusion.7), channel_id=1, replica_groups=mesh['dp'=16,'tensor'=16] {'tensor'}, use_global_device_ids=true, to_apply=%region_2.0 | all-reduce | flops 196608 | bytes 1179648 | tf_op jit(solution)/shard_map/psum | solution.py:73
  286.0 0.0 copy-start.5
  286.0 3.9 fusion.1
  290.0 0.0 copy-done.5
  290.0 2.0 fusion.30
  292.0 54.8 %all-reduce.8 = bf16[384,512]{1,0:T(8,128)(2,1)} all-reduce(f32[384,512]{1,0:T(8,128)} %fusion.30), channel_id=1, replica_groups=mesh['dp'=16,'tensor'=16] {'tensor'}, use_global_device_ids=true, to_apply=%region_3.0 | all-reduce | flops 196608 | bytes 1179648 | tf_op jit(solution)/shard_map/psum | solution.py:88
  346.9 2.0 fusion.31
  348.9 0.0 copy-done.2
  348.9 2.6 pad_maximum_fusion.1
  351.5 0.0 reduce-scatter.3.cloned.1.call-update
  351.5 0.2 reduce-scatter.5.cloned.1.call-start
  351.7 0.0 copy-start.1
  351.8 3.5 fusion.32
  355.3 0.0 copy-done.1
  355.3 1.4 fusion.2
  356.7 7.2 %pad_maximum_fusion = f32[512,4608]{1,0:T(8,128)} fusion(f32[512,2304]{1,0:T(8,128)S(1)} %fusion.2, f32[512,2304]{1,0:T(8,128)} %fusion.32), kind=kLoop, calls=%fused_computation | loop fusion | flops 2359296 | bytes 18874368 | tf_op jit(solution)/shard_map/concatenate | solution.py:81
  363.9 0.0 reduce-scatter.5.cloned.1.call-update
  364.0 0.0 copy-start.6
  364.0 0.0 copy-start.7
  364.0 0.0 copy-start.9
  364.0 0.0 copy-start.10
  364.0 69.9 %reduce-scatter.3.cloned.1.call-done = f32[32,2304]{1,0:T(8,128)} async-done(((f32[512,2304]{1,0:T(8,128)}), f32[32,2304]{1,0:T(8,128)}) %reduce-scatter.3.cloned.1.call-update) | async-done | bytes 294928 | tf_op jit(solution)/shard_map/reduce_scatter | solution.py:90
  434.0 1.6 multiply_reduce_fusion.3
  435.6 94.4 %reduce-scatter.5.cloned.1.call-done = f32[32,4608]{1,0:T(8,128)} async-done(((f32[512,4608]{1,0:T(8,128)}), f32[32,4608]{1,0:T(8,128)}) %reduce-scatter.5.cloned.1.call-update) | async-done | bytes 589840 | tf_op jit(solution)/shard_map/reduce_scatter | solution.py:80
  530.0 1.8 multiply_reduce_fusion.1
  534.4 76.7 %all-reduce = (f32[]{:T(128)}, f32[]{:T(128)}) all-reduce(f32[]{:T(128)S(6)} %add.63, f32[]{:T(128)} %get-tuple-element.27), channel_id=1, replica_groups=mesh['dp'=16,'tensor'=16] {'dp','tensor'}, use_global_device_ids=true, to_apply=%region_10.0 | all-reduce | flops 2 | bytes 16 | tf_op jit(solution)/shard_map/psum | solution.py:104
  612.5 0.0 copy-done.11
  612.5 0.0 copy-done.12
  612.5 2.2 divide_subtract_fusion.2
  614.6 0.9 pad_maximum_fusion.4
  615.5 0.0 copy-done.6
  615.5 0.0 copy-done.10
  615.5 0.0 copy-done.4
  615.5 1.2 divide_subtract_fusion
  616.8 1.1 pad_maximum_fusion.2
  (8 shorter events, 0.0 us)
Async XLA Ops:
  7.2 55.0 %copy-start = (bf16[384,1152]{1,0:T(8,128)(2,1)S(1)}, bf16[384,1152]{1,0:T(8,128)(2,1)}, u32[]{:S(2)}) copy-start(bf16[384,1152]{1,0:T(8,128)(2,1)} %param.10) | copy-start | bytes 2654212
  7.2 55.0 %all-gather.5.cloned.1.call-start = ((), (), s32[]{:S(2)}) async-start(), calls=%async_computation.2 | async-start | bytes 1253376 | tf_op jit(solution)/shard_map/all_gather | solution.py:51
  8.9 109.9 %all-gather.7.cloned.1.call-start = ((), (), s32[]{:S(2)}) async-start(), calls=%async_computation.3 | async-start | bytes 2506752 | tf_op jit(solution)/shard_map/all_gather | solution.py:52
  10.6 157.9 %all-gather.9.cloned.1.call-start = ((), (), s32[]{:S(2)}) async-start(), calls=%async_computation.4 | async-start | bytes 2506752 | tf_op jit(solution)/shard_map/all_gather | solution.py:53
  12.3 214.3 %all-gather.11.cloned.1.call-start = ((), (), s32[]{:S(2)}) async-start(), calls=%async_computation.5 | async-start | bytes 1253376 | tf_op jit(solution)/shard_map/all_gather | solution.py:54
  13.9 420.0 %reduce-scatter.3.cloned.1.call-start = ((), (), s32[]{:S(2)}) async-start(), calls=%async_computation.6 | async-start | bytes 5013504 | tf_op jit(solution)/shard_map/reduce_scatter | solution.py:90
  123.2 103.3 %copy-start.8 = (bf16[384,1152]{1,0:T(8,128)(2,1)S(1)}, bf16[384,1152]{1,0:T(8,128)(2,1)}, u32[]{:S(2)}) copy-start(bf16[384,1152]{1,0:T(8,128)(2,1)} %param.11) | copy-start | bytes 2654212
  229.2 2.3 copy-start.3
  286.0 4.0 copy-start.5
  346.9 2.0 copy-start.2
  351.5 178.5 %reduce-scatter.5.cloned.1.call-start = ((), (), s32[]{:S(2)}) async-start(), calls=%async_computation.7 | async-start | bytes 10027008 | tf_op jit(solution)/shard_map/reduce_scatter | solution.py:80
  351.7 3.5 copy-start.1
  363.9 248.5 %copy-start.11 = (f32[32,1152]{1,0:T(8,128)S(1)}, f32[32,1152]{1,0:T(8,128)}, u32[]{:S(2)}) copy-start(f32[32,1152]{1,0:T(8,128)} %param.15) | copy-start | bytes 442372
  363.9 248.5 %copy-start.12 = (f32[32,1152]{1,0:T(8,128)S(1)}, f32[32,1152]{1,0:T(8,128)}, u32[]{:S(2)}) copy-start(f32[32,1152]{1,0:T(8,128)} %param.12) | copy-start | bytes 442372
  364.0 251.5 %copy-start.6 = (f32[32,2304]{1,0:T(8,128)S(1)}, f32[32,2304]{1,0:T(8,128)}, u32[]{:S(2)}) copy-start(f32[32,2304]{1,0:T(8,128)} %param.13) | copy-start | bytes 884740
  364.0 251.5 %copy-start.7 = (f32[32,2304]{1,0:T(8,128)S(1)}, f32[32,2304]{1,0:T(8,128)}, u32[]{:S(2)}) copy-start(f32[32,2304]{1,0:T(8,128)} %param.14) | copy-start | bytes 884740
  364.0 251.5 %copy-start.9 = (f32[2,32,2304]{2,1,0:T(8,128)S(1)}, f32[2,32,2304]{2,1,0:T(8,128)}, u32[]{:S(2)}) copy-start(f32[2,32,2304]{2,1,0:T(8,128)} %param.18) | copy-start | bytes 1769476
  364.0 251.5 %copy-start.10 = (f32[2,32,2304]{2,1,0:T(8,128)S(1)}, f32[2,32,2304]{2,1,0:T(8,128)}, u32[]{:S(2)}) copy-start(f32[2,32,2304]{2,1,0:T(8,128)} %param.19) | copy-start | bytes 1769476
  530.0 85.5 %copy-start.4 = (f32[32,4608]{1,0:T(8,128)S(1)}, f32[32,4608]{1,0:T(8,128)}, u32[]{:S(2)}) copy-start(f32[32,4608]{1,0:T(8,128)} %reduce-scatter.5.cloned.1.call-done) | copy-start | bytes 1769476
Sparse Core Ops, SparseCore 0:
  11.1 51.0 all-gather.4
  65.2 50.0 all-gather.6
  118.4 50.0 all-gather.8
  171.4 47.5 all-gather.10
  351.6 82.2 reduce-scatter.2
  437.6 92.3 reduce-scatter.4
where the time goes:
time: 627 us; the launch traced here: 626 us
  blocking collectives  294 us (47%)
  waiting for transfers between devices  258 us (41%)
  matrix products  28.9 us (5%)
  other arithmetic  25.1 us (4%)
  between operations  19.4 us (3%)
    reduce_scatter x1, waiting for transfers between devices, shards(): lax.psum_scatter(jnp.concatenate([first_dims(rank_in, grad_pre), first_di...  94.4 us
    psum x1, blocking collectives, shards(): squares = lax.psum(local_squares, ('dp', 'tensor'))  76.7 us
    reduce_scatter x1, waiting for transfers between devices, shards(): lax.psum_scatter(jnp.concatenate([first_dims(grad_rank_in, tokens), first...  69.9 us
    psum x1, blocking collectives, shards(): lax.psum(last_dims(grad_pre, copy_po), 'tensor').astype(jnp.bfloat16)  54.8 us
    psum x1, blocking collectives, shards(): lax.psum(last_dims(tokens, copy_pi), 'tensor').astype(jnp.bfloat16)  54.6 us
    psum x1, blocking collectives, shards(): lax.psum(last_dims(hidden, copy_qi), 'tensor').astype(jnp.bfloat16)  54.2 us
    psum x1, blocking collectives, shards(): lax.psum(last_dims(grad_out, copy_qo), 'tensor').astype(jnp.bfloat16)  53.8 us
    all_gather x1, waiting for transfers between devices, shards(): lax.all_gather(copies[0], 'dp', axis=0, tiled=True)  48.2 us
  transfers between devices with their start and end apart: 6, of which 4 were waited for; matrix products, arithmetic and copies ran while one was open for 5% of the time, Pallas kernels for 0%

commit v1 on v0

v1 whole, which is shorter than its diff:
```python
import functools

import jax
import jax.numpy as jnp
from jax import lax
from jax.experimental import pallas as pl
from jax.experimental.pallas import tpu as pltpu
from jax.sharding import PartitionSpec as P

beta_one = 0.9
beta_two = 0.95
learn_rate = 0.1
tiny_eps = 1e-08

MESH = pl.DeviceIdType.MESH
BF = jnp.bfloat16
F32 = jnp.float32

NX, NY, NZ = 4, 4, 8
DP = NX * NY
TP = NZ * 2
ROWS = 32
RANK = DP * ROWS
TOKD = 384
HALF = TOKD // 2
TOTAL = TOKD * DP
PI, PO, QI, QO = 0, 1, 2, 3


def dot_nt(left, right):
    return lax.dot_general(
        left, right, (((1,), (1,)), ((), ())), preferred_element_type=F32
    )


def dot_nn(left, right):
    return jnp.dot(left, right, preferred_element_type=F32)


def body(
    tokens, target, fi, fo, si, so,
    g_pi, g_po, g_qi, g_qo, stat,
    tok, tgt, wf0, wf1, wf2, wf3,
    w0, w1, w2, w3, gr0, gr1, gr2, gr3,
    ra0, ra1, ra2, ra3, rb0, rb1, rb2, rb3, rc0, rc1, rc2, rc3,
    rank, ranks_t, relu, hid, gpre, gout, partial,
    sib_send, sib_recv, z_keep, z_send, z_recv, loss_acc, sc_buf,
    ld_sem, ag_send, ag_recv, rs_send, rs_recv, ar_send, ar_recv, sc_send, sc_recv,
):
    me_dp = lax.axis_index("dp")
    me_t = lax.axis_index("tensor")
    x, y = me_dp // NY, lax.rem(me_dp, NY)
    z, c = me_t // 2, lax.rem(me_t, 2)
    wf = (wf0, wf1, wf2, wf3)
    w = (w0, w1, w2, w3)
    gr = (gr0, gr1, gr2, gr3)
    ra = (ra0, ra1, ra2, ra3)
    rb = (rb0, rb1, rb2, rb3)
    rc = (rc0, rc1, rc2, rc3)
    gouts = (g_pi, g_po, g_qi, g_qo)
    cols = tuple(r.shape[-1] for r in wf)

    def at_x(d):
        return (lax.rem(x + d, NX) * NY + y, me_t)

    def at_y(d):
        return (x * NY + lax.rem(y + d, NY), me_t)

    def at_z(d):
        return (me_dp, lax.rem(z + d, NZ) * 2 + c)

    sibling = (me_dp, z * 2 + 1 - c)

    def send(src, dst, s_sem, r_sem, where):
        pltpu.make_async_remote_copy(
            src_ref=src, dst_ref=dst, send_sem=s_sem, recv_sem=r_sem,
            device_id=where, device_id_type=MESH,
        ).start()

    def wait_for(ref, sem):
        pltpu.make_async_copy(ref, ref, sem).wait()

    loads = [
        pltpu.make_async_copy(s, d, ld_sem.at[k])
        for k, (s, d) in enumerate(
            ((fi, wf0), (fo, wf1), (tokens, tok), (si, wf2), (so, wf3), (target, tgt))
        )
    ]
    for cp in loads:
        cp.start()

    barrier = pltpu.get_barrier_semaphore()

    def greet(k, carry):
        pl.semaphore_signal(
            barrier, inc=1, device_id=(lax.rem(me_dp + k, DP), me_t), device_id_type=MESH
        )
        pl.semaphore_signal(
            barrier, inc=1, device_id=(me_dp, lax.rem(me_t + k, TP)), device_id_type=MESH
        )
        return carry

    lax.fori_loop(1, DP, greet, 0)

    def cast(a):
        w[a][x, y] = wf[a][...].astype(BF).reshape(2, 16, cols[a])

    def gather_one(a):
        for d in (2, 1, 3):
            own = w[a].at[x, y, 0]
            send(own, own, ag_send.at[a, 0, 0], ag_recv.at[a, 0, 0], at_x(d))
            own = w[a].at[x, y, 1]
            send(own, own, ag_send.at[a, 0, 1], ag_recv.at[a, 0, 1], at_y(d))

    def gather_two(a):
        wait_for(w[a].at[pl.ds(0, 3), 0, 0], ag_recv.at[a, 0, 0])
        for d in (2, 1, 3):
            part = w[a].at[:, y, 0]
            send(part, part, ag_send.at[a, 1, 0], ag_recv.at[a, 1, 0], at_y(d))
        wait_for(w[a].at[0, pl.ds(0, 3), 1], ag_recv.at[a, 0, 1])
        for d in (2, 1, 3):
            part = w[a].at[x, :, 1]
            send(part, part, ag_send.at[a, 1, 1], ag_recv.at[a, 1, 1], at_x(d))

    def gather_end(a):
        wait_for(w[a].at[:, pl.ds(0, 3), 0], ag_recv.at[a, 1, 0])
        wait_for(w[a].at[pl.ds(0, 3), :, 1], ag_recv.at[a, 1, 1])

    def sum_send(s, h, left, a):
        n = 1 - c
        sib_send[s, h] = dot_nt(left, w[a][pl.ds(2 * n, 2)].reshape(256, cols[a])).astype(BF)
        send(sib_send.at[s, h], sib_recv.at[s, h], ar_send.at[s, h, 0], ar_recv.at[s, h, 0], sibling)
        partial[h] = dot_nt(left, w[a][pl.ds(2 * c, 2)].reshape(256, cols[a]))

    def sum_scatter(s, h):
        wait_for(sib_recv.at[s, h], ar_recv.at[s, h, 0])
        both = partial[h] + sib_recv[s, h].astype(F32)
        for k in range(NZ):
            zr, zc = k // 2, k % 2
            piece = both[zr * 48 : (zr + 1) * 48, zc * 128 : (zc + 1) * 128]
            z_keep[h, k] = piece
            z_send[s, h, k] = piece.astype(BF)

        def one(i, carry):
            d = lax.rem(i + 3, NZ - 1) + 1
            send(
                z_send.at[s, h, lax.rem(z + d, NZ)], z_recv.at[s, h, d - 1],
                ar_send.at[s, h, 1], ar_recv.at[s, h, 1], at_z(d),
            )
            return carry

        lax.fori_loop(0, NZ - 1, one, 0)

    def spot(s, h):
        row = pl.multiple_of(h * HALF + (z // 2) * 48, 16)
        col = pl.multiple_of(c * 256 + lax.rem(z, 2) * 128, 128)
        return rank.at[s, pl.ds(row, 48), pl.ds(col, 128)]

    def sum_gather(s, h):
        wait_for(z_recv.at[s, h], ar_recv.at[s, h, 1])
        total = z_keep[h, z]
        for k in range(NZ - 1):
            total = total + z_recv[s, h, k].astype(F32)
        mine = spot(s, h)
        mine[...] = total.astype(BF)

        def one(i, carry):
            d = lax.rem(i + 3, NZ - 1) + 1
            send(mine, mine, ar_send.at[s, h, 2], ar_recv.at[s, h, 2], at_z(d))
            return carry

        lax.fori_loop(0, NZ - 1, one, 0)

    def half_of(s, h):
        col = pl.multiple_of(c * 256, 128)
        return rank.at[s, pl.ds(h * HALF, HALF), pl.ds(col, 256)]

    def sum_share(s, h):
        wait_for(z_recv.at[s, h], ar_recv.at[s, h, 2])
        part = half_of(s, h)
        send(part, part, ar_send.at[s, h, 3], ar_recv.at[s, h, 3], sibling)

    def sum_end(s, h):
        wait_for(half_of(s, h), ar_recv.at[s, h, 3])

    def scatter_one(a):
        for d in (2, 1, 3):
            send(
                gr[a].at[:, lax.rem(y + d, NY), 0], ra[a].at[0, d - 1],
                rs_send.at[a, 0, 0], rs_recv.at[a, 0, 0], at_y(d),
            )
            send(
                gr[a].at[lax.rem(x + d, NX), :, 1], ra[a].at[1, d - 1],
                rs_send.at[a, 0, 1], rs_recv.at[a, 0, 1], at_x(d),
            )

    def scatter_two(a):
        for half in range(2):
            wait_for(ra[a].at[half], rs_recv.at[a, 0, half])

            def one(k, carry):
                own = gr[a][k, y, 0] if half == 0 else gr[a][x, k, 1]
                total = own.astype(F32)
                for j in range(3):
                    total = total + ra[a][half, j, k].astype(F32)
                rb[a][half, k] = total.astype(BF)
                return carry

            lax.fori_loop(0, 4, one, 0)
            for d in (2, 1, 3):
                if half == 0:
                    there, where = lax.rem(x + d, NX), at_x(d)
                else:
                    there, where = lax.rem(y + d, NY), at_y(d)
                send(
                    rb[a].at[half, there], rc[a].at[half, d - 1],
                    rs_send.at[a, 1, half], rs_recv.at[a, 1, half], where,
                )

    def scatter_end(a):
        squares = jnp.zeros((8, 128), F32)
        for half in range(2):
            wait_for(rc[a].at[half], rs_recv.at[a, 1, half])
            total = rb[a][half, x if half == 0 else y].astype(F32)
            for j in range(3):
                total = total + rc[a][half, j].astype(F32)
            gouts[a][half * 16 : (half + 1) * 16, :] = total
            sq = total * total
            sq = sq[0:8] + sq[8:16]
            for j in range(cols[a] // 128):
                squares = squares + sq[:, j * 128 : (j + 1) * 128]
        return squares

    def gradient(a, s, right):
        ranks_t[...] = rank[s].T
        step = 256 if cols[a] % 256 == 0 else 384

        def one(j, carry):
            at = pl.ds(pl.multiple_of(j * step, 128), step)
            tile = dot_nn(ranks_t[...], right[:, at]).astype(BF)
            gr[a][:, :, :, :, at] = tile.reshape(NX, NY, 2, 16, step)
            return carry

        lax.fori_loop(0, cols[a] // step, one, 0)

    def tile_of(a, at, n):
        return w[a][:, :, :, :, at].reshape(RANK, n)

    def rows_of(h):
        return pl.ds(h * HALF, HALF)

    def stage_zero(h):
        sum_send(0, h, tok[rows_of(h), :], PI)

    def stage_one(h):
        left = rank[0, rows_of(h), :]

        def one(j, carry):
            at = pl.ds(pl.multiple_of(j * 256, 128), 256)
            pre = jnp.maximum(dot_nn(left, tile_of(PO, at, 256)), 0.0)
            relu[rows_of(h), at] = pre
            hid[rows_of(h), at] = (pre * pre).astype(BF)
            return carry

        lax.fori_loop(0, cols[PO] // 256, one, 0)

    def stage_two(h):
        left = rank[1, rows_of(h), :]

        def one(j, carry):
            at = pl.ds(pl.multiple_of(j * 384, 128), 384)
            misfit = dot_nn(left, tile_of(QO, at, 384)) - tgt[rows_of(h), at].astype(F32)
            gout[rows_of(h), at] = (misfit * (1.0 / TOTAL)).astype(BF)
            sq = (misfit * misfit).reshape(HALF // 8, 8, 384).sum(axis=0)
            loss_acc[...] += sq[:, 0:128] + sq[:, 128:256] + sq[:, 256:384]
            return carry

        lax.fori_loop(0, cols[QO] // 384, one, 0)

    def stage_three(h):
        left = rank[2, rows_of(h), :]

        def one(j, carry):
            at = pl.ds(pl.multiple_of(j * 256, 128), 256)
            up = dot_nn(left, tile_of(QI, at, 256))
            gpre[rows_of(h), at] = (up * 2.0 * relu[rows_of(h), at]).astype(BF)
            return carry

        lax.fori_loop(0, cols[QI] // 256, one, 0)

    loss_acc[...] = jnp.zeros_like(loss_acc)
    loads[0].wait()
    cast(PI)
    pl.semaphore_wait(barrier, 2 * (DP - 1))
    gather_one(PI)
    loads[1].wait()
    cast(PO)
    gather_one(PO)
    loads[3].wait()
    cast(QI)
    loads[4].wait()
    cast(QO)
    gather_two(PI)
    gather_two(PO)
    gather_one(QI)
    gather_one(QO)
    loads[2].wait()
    loads[5].wait()
    gather_end(PI)
    stage_zero(0)
    stage_zero(1)
    sum_scatter(0, 0)
    sum_scatter(0, 1)
    gather_two(QI)
    sum_gather(0, 0)
    sum_gather(0, 1)
    gather_two(QO)
    sum_share(0, 0)
    sum_share(0, 1)
    gather_end(PO)
    sum_end(0, 0)
    stage_one(0)
    gather_end(QI)
    sum_send(1, 0, hid[rows_of(0), :], QI)
    sum_end(0, 1)
    stage_one(1)
    sum_send(1, 1, hid[rows_of(1), :], QI)
    sum_scatter(1, 0)
    sum_scatter(1, 1)
    sum_gather(1, 0)
    sum_gather(1, 1)
    sum_share(1, 0)
    sum_share(1, 1)
    gather_end(QO)
    sum_end(1, 0)
    stage_two(0)
    sum_send(2, 0, gout[rows_of(0), :], QO)
    sum_end(1, 1)
    stage_two(1)
    sum_send(2, 1, gout[rows_of(1), :], QO)
    sum_scatter(2, 0)
    sum_scatter(2, 1)
    gradient(QO, 1, gout)
    scatter_one(QO)
    sum_gather(2, 0)
    sum_gather(2, 1)
    sum_share(2, 0)
    sum_share(2, 1)
    sum_end(2, 0)
    sum_end(2, 1)
    gradient(QI, 2, hid)
    scatter_one(QI)
    stage_three(0)
    sum_send(3, 0, gpre[rows_of(0), :], PO)
    stage_three(1)
    sum_send(3, 1, gpre[rows_of(1), :], PO)
    sum_scatter(3, 0)
    sum_scatter(3, 1)
    gradient(PO, 0, gpre)
    scatter_one(PO)
    sum_gather(3, 0)
    sum_gather(3, 1)
    scatter_two(QO)
    sum_share(3, 0)
    sum_share(3, 1)
    sum_end(3, 0)
    sum_end(3, 1)
    gradient(PI, 3, tok)
    scatter_one(PI)
    scatter_two(QI)
    scatter_two(PO)
    scatter_two(PI)
    squares = scatter_end(QO)
    squares = squares + scatter_end(QI)
    squares = squares + scatter_end(PO)
    squares = squares + scatter_end(PI)

    sc_buf[0, me_t, 0] = squares
    sc_buf[0, me_t, 1] = loss_acc[...]

    def over_tensor(k, carry):
        own = sc_buf.at[0, me_t]
        send(own, own, sc_send.at[0], sc_recv.at[0], (me_dp, lax.rem(me_t + k, TP)))
        return carry

    lax.fori_loop(1, TP, over_tensor, 0)
    wait_for(sc_buf.at[0, pl.ds(0, TP - 1)], sc_recv.at[0])
    sc_buf[1, me_dp] = jnp.sum(sc_buf[0], axis=0)

    def over_dp(k, carry):
        own = sc_buf.at[1, me_dp]
        send(own, own, sc_send.at[1], sc_recv.at[1], (lax.rem(me_dp + k, DP), me_t))
        return carry

    lax.fori_loop(1, DP, over_dp, 0)
    wait_for(sc_buf.at[1, pl.ds(0, DP - 1)], sc_recv.at[1])
    stat[...] = jnp.sum(sc_buf[1], axis=0)

    for a in range(4):
        for half in range(2):
            wait_for(w[a].at[pl.ds(0, 3), 0, 0], ag_send.at[a, 0, half])
            wait_for(w[a].at[:, pl.ds(0, 3), 0], ag_send.at[a, 1, half])
            wait_for(ra[a].at[half], rs_send.at[a, 0, half])
            wait_for(rc[a].at[half], rs_send.at[a, 1, half])
    for s in range(4):
        for h in range(2):
            wait_for(sib_recv.at[s, h], ar_send.at[s, h, 0])
            wait_for(z_recv.at[s, h], ar_send.at[s, h, 1])
            wait_for(z_recv.at[s, h], ar_send.at[s, h, 2])
            wait_for(sib_recv.at[s, h], ar_send.at[s, h, 3])
    for k in range(2):
        wait_for(sc_buf.at[k, pl.ds(0, TP - 1)], sc_send.at[k])


def adam_body(
    stat, g_pi, g_po, g_qi, g_qo, p_pi, p_po, p_qi, p_qo, wm, ws, hm, hs,
    n_pi, n_po, n_qi, n_qo, nwm, nws, nhm, nhs, loss,
):
    squares = jnp.sum(stat[0])
    scale = 1.0 / jnp.maximum(jnp.sqrt(squares), 1.0)
    loss[0, 0] = jnp.sum(stat[1]) / (2.0 * TOTAL)
    for g, p, m, v, k, new_p, new_m, new_v in (
        (g_pi, p_pi, wm, ws, 0, n_pi, nwm, nws),
        (g_qo, p_qo, wm, ws, 1, n_qo, nwm, nws),
        (g_po, p_po, hm, hs, 0, n_po, nhm, nhs),
        (g_qi, p_qi, hm, hs, 1, n_qi, nhm, nhs),
    ):
        grad = g[...] * scale
        mean = beta_one * m[k] + (1.0 - beta_one) * grad
        square = beta_two * v[k] + (1.0 - beta_two) * grad * grad
        corrected = mean * (1.0 / (1.0 - beta_one**10))
        spread = jnp.sqrt(square * (1.0 / (1.0 - beta_two**10))) + tiny_eps
        new_p[...] = p[...] - learn_rate * corrected / spread
        new_m[k] = mean
        new_v[k] = square


def shards(
    tokens, target, first_in, first_out, second_in, second_out,
    width_mean, width_square, hidden_mean, hidden_square,
):
    wide = first_in.shape[1]
    deep = first_out.shape[1]
    cols = (wide, deep, deep, wide)
    vm = pltpu.VMEM
    dma = pltpu.SemaphoreType.DMA
    scratch = [vm((TOKD, wide), BF), vm((TOKD, wide), BF)]
    scratch += [vm((ROWS, n), F32) for n in cols]
    scratch += [vm((NX, NY, 2, 16, n), BF) for n in cols]
    scratch += [vm((NX, NY, 2, 16, n), BF) for n in cols]
    scratch += [vm((2, 3, 4, 16, n), BF) for n in cols]
    scratch += [vm((2, 4, 16, n), BF) for n in cols]
    scratch += [vm((2, 3, 16, n), BF) for n in cols]
    scratch += [
        vm((4, TOKD, RANK), BF),
        vm((RANK, TOKD), BF),
        vm((TOKD, deep), F32),
        vm((TOKD, deep), BF),
        vm((TOKD, deep), BF),
        vm((TOKD, wide), BF),
        vm((2, HALF, 256), F32),
        vm((4, 2, HALF, 256), BF),
        vm((4, 2, HALF, 256), BF),
        vm((2, NZ, 48, 128), F32),
        vm((4, 2, NZ, 48, 128), BF),
        vm((4, 2, NZ - 1, 48, 128), BF),
        vm((8, 128), F32),
        vm((2, 16, 2, 8, 128), F32),
        dma((6,)),
        dma((4, 2, 2)), dma((4, 2, 2)),
        dma((4, 2, 2)), dma((4, 2, 2)),
        dma((4, 2, 4)), dma((4, 2, 4)),
        dma((2,)), dma((2,)),
    ]
    whole = pl.BlockSpec(memory_space=pltpu.VMEM)
    g_pi, g_po, g_qi, g_qo, stat = pl.pallas_call(
        body,
        name="step",
        out_shape=[jax.ShapeDtypeStruct((ROWS, n), F32) for n in cols]
        + [jax.ShapeDtypeStruct((2, 8, 128), F32)],
        in_specs=[pl.BlockSpec(memory_space=pl.ANY)] * 6,
        out_specs=[whole] * 5,
        scratch_shapes=scratch,
        compiler_params=pltpu.CompilerParams(
            collective_id=0, has_side_effects=True, vmem_limit_bytes=58 * 2**20
        ),
    )(tokens, target, first_in, first_out, second_in, second_out)

    steps = 3
    w2 = pl.BlockSpec((ROWS, wide // steps), lambda i: (0, i))
    h2 = pl.BlockSpec((ROWS, deep // steps), lambda i: (0, i))
    w3 = pl.BlockSpec((2, ROWS, wide // steps), lambda i: (0, 0, i))
    h3 = pl.BlockSpec((2, ROWS, deep // steps), lambda i: (0, 0, i))
    outs = pl.pallas_call(
        adam_body,
        name="adam",
        grid=(steps,),
        out_shape=[jax.ShapeDtypeStruct((ROWS, n), F32) for n in cols]
        + [jax.ShapeDtypeStruct((2, ROWS, n), F32) for n in (wide, wide, deep, deep)]
        + [jax.ShapeDtypeStruct((1, 1), F32)],
        in_specs=[
            pl.BlockSpec((2, 8, 128), lambda i: (0, 0, 0)),
            w2, h2, h2, w2, w2, h2, h2, w2, w3, w3, h3, h3,
        ],
        out_specs=[
            w2, h2, h2, w2, w3, w3, h3, h3,
            pl.BlockSpec((1, 1), lambda i: (0, 0), memory_space=pltpu.SMEM),
        ],
        compiler_params=pltpu.CompilerParams(vmem_limit_bytes=40 * 2**20),
    )(
        stat, g_pi, g_po, g_qi, g_qo, first_in, first_out, second_in, second_out,
        width_mean, width_square, hidden_mean, hidden_square,
    )
    return tuple(outs[:8]) + (outs[8].reshape(()),)


def solution(mesh):
    two = P("dp", "tensor")
    three = P(None, "dp", "tensor")
    return jax.shard_map(
        shards,
        mesh=mesh,
        in_specs=(two,) * 6 + (three,) * 4,
        out_specs=(two,) * 4 + (three,) * 4 + (P(),),
        check_vma=False,
    )
```

time: 627 us -> 159 us (0.25)
  blocking collectives: 294 us -> 0 us
  waiting for transfers between devices: 258 us -> 0 us
  Pallas kernels: 0 us -> 154 us
  matrix products: 28.9 us -> 0 us
  other arithmetic: 25.1 us -> 0 us
  between operations: 19.4 us -> 0.79 us
    psum x5 -> x0, blocking collectives: 294 us -> none  [the longest x1 76.7 us: shards(): squares = lax.psum(local_squares, ('dp', 'tensor'))]
    reduce_scatter x2 -> x0, waiting for transfers between devices: 164 us -> none  [the longest x1 94.4 us: shards(): lax.psum_scatter(jnp.concatenate([first_dims(rank_in, grad_pre), first_di...]
    pallas_call x0 -> x2, Pallas kernels: none -> 154 us  [the longest x1 151 us: shards(): pl.pallas_call(body, name='step', out_shape=[jax.ShapeDtypeStruct((ROWS,...]
    all_gather x4 -> x0, waiting for transfers between devices: 93.5 us -> none  [the longest x1 48.2 us: shards(): lax.all_gather(copies[0], 'dp', axis=0, tiled=True)]
    dot_general x11 -> x0, matrix products: 28.9 us -> none  [the longest x4 9.3 us: first_dims(): lax.dot_general(left, right, (((0,), (0,)), ((), ())), preferred_element_...]
    concatenate x2 -> x0, other arithmetic: 9.83 us -> none  [the longest x1 7.22 us: shards(): jnp.concatenate([first_dims(rank_in, grad_pre), first_dims(grad_rank_out,...]
    convert_element_type x4 -> x0, other arithmetic: 6.46 us -> none  [the longest x1 1.64 us: shards(): second_in.astype(jnp.bfloat16)]
  transfers between devices with their start and end apart: 6 -> 0, of which waited for: 4 -> 0; matrix products, arithmetic and copies ran while one was open for 5% -> 0% of each run, Pallas kernels for 0% -> 0%
where the time goes in v1:
time: 159 us
  Pallas kernels  154 us (97%)
  local copies, waits for them, and re-layouts  4.38 us (3%)
    pallas_call x1, Pallas kernels, shards(): pl.pallas_call(body, name='step', out_shape=[jax.ShapeDtypeStruct((ROWS,...  151 us
    unnamed x26, local copies, waits for them, and re-layouts  4.38 us

profile of v1, /device:TPU:1, one launch (start us, length us, event | category | flops | bytes accessed | tf_op | source)
XLA Modules:
  0.0 158.9 jit_solution(13468654350201537650)
XLA Ops:
  0.6 0.0 copy-start.5
  0.7 0.0 copy-start.1
  0.7 0.0 copy-start
  0.7 0.0 copy-start.4
  0.7 0.0 copy-start.3
  0.7 0.0 copy-start.2
  0.7 0.0 copy-start.7
  0.7 0.0 copy-start.6
  0.7 151.0 %step.1 = (f32[32,1152]{1,0:T(8,128)}, f32[32,2304]{1,0:T(8,128)}, f32[32,2304]{1,0:T(8,128)}, f32[32,1152]{1,0:T(8,128)}, f32[2,8,128]{2,1,0:T(8,128)}) custom-call(bf16[384,1152]{1,0:T(8,128)(2,1)} %tokens.1, bf16[384,1152]{1,0:T(8,128)(2,1)} %target.1, f32[32,1152]{1,0:T(8,128)} %p_pi.1, f32[32,2304]{1,0:T(8,128)} %p_po.1, f32[32,2304]{1,0:T(8,128)} %p_qi.1, ...), custom_call_target="tpu_custom_call" | custom-call | tf_op jit(solution)/shard_map/step/pallas_call | solution.py:476
  151.7 0.0 copy-start.12
  151.7 0.0 copy-done.5
  151.7 0.0 copy-done.1
  151.7 0.0 copy-done
  151.7 0.0 copy-done.4
  151.7 0.0 copy-done.3
  151.8 0.0 copy-done.2
  151.8 0.0 copy-done.7
  151.8 0.0 copy-done.6
  151.8 0.6 copy-done.12
  152.4 0.0 copy-start.8
  152.4 1.0 copy-done.8
  153.4 0.0 copy-start.9
  153.4 1.0 copy-done.9
  154.3 0.0 copy-start.10
  154.3 0.9 copy-done.10
  155.2 0.0 copy-start.11
  155.2 0.9 copy-done.11
  156.1 2.7 %adam.1 = (f32[32,1152]{1,0:T(8,128)}, f32[32,2304]{1,0:T(8,128)}, f32[32,2304]{1,0:T(8,128)}, f32[32,1152]{1,0:T(8,128)}, f32[2,32,1152]{2,1,0:T(8,128)}, /*ind...) custom-call(f32[2,8,128]{2,1,0:T(8,128)S(1)} %copy-done.12, ...), custom_call_target="tpu_custom_call" | custom-call | tf_op jit(solution)/shard_map/adam/pallas_call | solution.py:494
Async XLA Ops:
  0.6 151.1 %copy-start.5 = (f32[32,1152]{1,0:T(8,128)S(1)}, f32[32,1152]{1,0:T(8,128)}, u32[]{:S(2)}) copy-start(f32[32,1152]{1,0:T(8,128)} %p_qo.1) | copy-start | bytes 442372
  0.7 151.1 %copy-start.1 = (f32[32,2304]{1,0:T(8,128)S(1)}, f32[32,2304]{1,0:T(8,128)}, u32[]{:S(2)}) copy-start(f32[32,2304]{1,0:T(8,128)} %p_qi.1) | copy-start | bytes 884740
  0.7 151.1 %copy-start = (f32[32,2304]{1,0:T(8,128)S(1)}, f32[32,2304]{1,0:T(8,128)}, u32[]{:S(2)}) copy-start(f32[32,2304]{1,0:T(8,128)} %p_po.1) | copy-start | bytes 884740
  0.7 151.1 %copy-start.4 = (f32[32,1152]{1,0:T(8,128)S(1)}, f32[32,1152]{1,0:T(8,128)}, u32[]{:S(2)}) copy-start(f32[32,1152]{1,0:T(8,128)} %p_pi.1) | copy-start | bytes 442372
  0.7 151.1 %copy-start.3 = (f32[2,32,2304]{2,1,0:T(8,128)S(1)}, f32[2,32,2304]{2,1,0:T(8,128)}, u32[]{:S(2)}) copy-start(f32[2,32,2304]{2,1,0:T(8,128)} %hs.1) | copy-start | bytes 1769476
  0.7 151.1 %copy-start.2 = (f32[2,32,2304]{2,1,0:T(8,128)S(1)}, f32[2,32,2304]{2,1,0:T(8,128)}, u32[]{:S(2)}) copy-start(f32[2,32,2304]{2,1,0:T(8,128)} %hm.1) | copy-start | bytes 1769476
  0.7 151.1 %copy-start.7 = (f32[2,32,1152]{2,1,0:T(8,128)S(1)}, f32[2,32,1152]{2,1,0:T(8,128)}, u32[]{:S(2)}) copy-start(f32[2,32,1152]{2,1,0:T(8,128)} %ws.1) | copy-start | bytes 884740
  0.7 151.1 %copy-start.6 = (f32[2,32,1152]{2,1,0:T(8,128)S(1)}, f32[2,32,1152]{2,1,0:T(8,128)}, u32[]{:S(2)}) copy-start(f32[2,32,1152]{2,1,0:T(8,128)} %wm.1) | copy-start | bytes 884740
  151.7 0.7 copy-start.12
  152.4 1.0 copy-start.8
  153.4 1.0 copy-start.9
  154.3 0.9 copy-start.10
  155.2 0.9 copy-start.11

commit v2 on v1

v2 whole, which is shorter than its diff:
```python
import functools

import jax
import jax.numpy as jnp
from jax import lax
from jax.experimental import pallas as pl
from jax.experimental.pallas import tpu as pltpu
from jax.sharding import PartitionSpec as P

beta_one = 0.9
beta_two = 0.95
learn_rate = 0.1
tiny_eps = 1e-08

MESH = pl.DeviceIdType.MESH
BF = jnp.bfloat16
F32 = jnp.float32

NX, NY, NZ = 4, 4, 8
DP = NX * NY
TP = NZ * 2
ROWS = 32
RANK = DP * ROWS
TOKD = 384
HALF = TOKD // 2
TOTAL = TOKD * DP
PI, PO, QI, QO = 0, 1, 2, 3
GRAM = 4


def dot_nt(left, right):
    return lax.dot_general(
        left, right, (((1,), (1,)), ((), ())), preferred_element_type=F32
    )


def dot_nn(left, right):
    return jnp.dot(left, right, preferred_element_type=F32)


def body(
    tokens, target, fi, fo, si, so,
    g_pi, g_po, g_qi, g_qo, stat,
    tok, tgt, wf0, wf1, wf2, wf3,
    w0, w1, w2, w3, gr0, gr1, gr2, gr3,
    ra0, ra1, ra2, ra3, rb0, rb1, rb2, rb3, rc0, rc1, rc2, rc3,
    cb0, cb1, cb2, cb3,
    rank, back, ranks_t, relu, hid, gpre, gout, partial,
    sib_send, sib_recv, z_keep, z_send, z_recv,
    gram, gpartial, gsib_send, gsib_recv, gz_keep, gz_send, gz_recv, loss_acc, sc_buf,
    ld_sem, ag_send, ag_recv, rs_send, rs_recv, ar_send, ar_recv, sc_send, sc_recv,
):
    me_dp = lax.axis_index("dp")
    me_t = lax.axis_index("tensor")
    x, y = me_dp // NY, lax.rem(me_dp, NY)
    z, c = me_t // 2, lax.rem(me_t, 2)
    wf = (wf0, wf1, wf2, wf3)
    w = (w0, w1, w2, w3)
    gr = (gr0, gr1, gr2, gr3)
    ra = (ra0, ra1, ra2, ra3)
    rb = (rb0, rb1, rb2, rb3)
    rc = (rc0, rc1, rc2, rc3)
    cb = (cb0, cb1, cb2, cb3)
    gouts = (g_pi, g_po, g_qi, g_qo)
    cols = tuple(r.shape[-1] for r in wf)

    def at_x(d):
        return (lax.rem(x + d, NX) * NY + y, me_t)

    def at_y(d):
        return (x * NY + lax.rem(y + d, NY), me_t)

    def at_z(d):
        return (me_dp, lax.rem(z + d, NZ) * 2 + c)

    sibling = (me_dp, z * 2 + 1 - c)

    sent = []

    def start(src, dst, s_sem, r_sem, where):
        pltpu.make_async_remote_copy(
            src_ref=src, dst_ref=dst, send_sem=s_sem, recv_sem=r_sem,
            device_id=where, device_id_type=MESH,
        ).start()

    def send(src, dst, sems, spot_of, where):
        start(src, dst, sems[0].at[spot_of], sems[1].at[spot_of], where)
        sent.append((src, sems[0], spot_of))

    def wait_for(ref, sem, spot_of):
        at = sem.at[spot_of]
        pltpu.make_async_copy(ref, ref, at).wait()

    ag = (ag_send, ag_recv)
    rs = (rs_send, rs_recv)
    ar = (ar_send, ar_recv)
    low, high = pl.ds(0, 2), pl.ds(2, 2)

    def around(m):
        return lax.rem(m + 1, 4), lax.rem(m + 2, 4), lax.rem(m + 3, 4)

    loads = [
        pltpu.make_async_copy(s, d, ld_sem.at[k])
        for k, (s, d) in enumerate(
            ((fi, wf0), (fo, wf1), (tokens, tok), (si, wf2), (so, wf3), (target, tgt))
        )
    ]
    for cp in loads:
        cp.start()

    barrier = pltpu.get_barrier_semaphore()

    def greet(k, carry):
        pl.semaphore_signal(
            barrier, inc=1, device_id=(lax.rem(me_dp + k, DP), me_t), device_id_type=MESH
        )
        pl.semaphore_signal(
            barrier, inc=1, device_id=(me_dp, lax.rem(me_t + k, TP)), device_id_type=MESH
        )
        return carry

    lax.fori_loop(1, DP, greet, 0)

    def cast(a):
        w[a][x, y] = wf[a][...].astype(BF).reshape(2, 16, cols[a])

    def slot(a, half, p, q, part=slice(None)):
        if half == 0:
            return w[a].at[p, q, 0, :, part]
        return w[a].at[q, p, 1, :, part]

    def places(half):
        return (x, y, at_x, at_y) if half == 0 else (y, x, at_y, at_x)

    def gather_one(a):
        for half in range(2):
            m, q, go, _ = places(half)
            own = slot(a, half, m, q)
            for d in (2, 1, 3):
                send(own, own, ag, (a, 0, half, d - 1), go(d))

    def gather_two(a):
        for half in range(2):
            m, q, _, go = places(half)
            for d in range(3):
                wait_for(slot(a, half, m, q), ag_recv, (a, 0, half, d))
            row = slot(a, half, pl.ds(0, 4), q)
            send(row, row, ag, (a, 1, half, 0), go(1))
            send(row, row, ag, (a, 1, half, 1), go(3))

    def gather_last(a):
        for half in range(2):
            _, q, _, go = places(half)
            right, _, left = around(q)
            wait_for(slot(a, half, pl.ds(0, 4), left), ag_recv, (a, 1, half, 0))
            part = slot(a, half, low, left)
            send(part, part, ag, (a, 2, half, 0), go(1))
            wait_for(slot(a, half, pl.ds(0, 4), right), ag_recv, (a, 1, half, 1))
            part = slot(a, half, high, right)
            send(part, part, ag, (a, 2, half, 1), go(3))

    def gather_end(a):
        for half in range(2):
            _, q, _, _ = places(half)
            _, far, _ = around(q)
            wait_for(slot(a, half, low, far), ag_recv, (a, 2, half, 0))
            wait_for(slot(a, half, high, far), ag_recv, (a, 2, half, 1))

    def set_of(s):
        if s == GRAM:
            return gsib_send, gsib_recv, gz_keep, gz_send, gz_recv, gram, gpartial
        return (
            sib_send.at[s], sib_recv.at[s], z_keep.at[s], z_send.at[s], z_recv.at[s], rank.at[s], partial,
        )

    def sum_send(s, h, left, a):
        out, into, _, _, _, _, keep = set_of(s)
        n = 1 - c
        out[h] = dot_nt(left, w[a][pl.ds(2 * n, 2)].reshape(256, cols[a])).astype(BF)
        send(out.at[h], into.at[h], ar, (s, h, 0), sibling)
        keep[h] = dot_nt(left, w[a][pl.ds(2 * c, 2)].reshape(256, cols[a]))

    def sum_scatter(s, h):
        _, into, own, out, there, _, keep = set_of(s)
        tall = out.shape[2]
        wait_for(into.at[h], ar_recv, (s, h, 0))
        both = keep[h] + into[h].astype(F32)
        for k in range(NZ):
            zr, zc = k // 2, k % 2
            piece = both[zr * tall : (zr + 1) * tall, zc * 128 : (zc + 1) * 128]
            own[h, k] = piece
            out[h, k] = piece.astype(BF)

        def one(i, carry):
            d = lax.rem(i + 3, NZ - 1) + 1
            start(
                out.at[h, lax.rem(z + d, NZ)], there.at[h, d - 1],
                ar_send.at[s, h, 1], ar_recv.at[s, h, 1], at_z(d),
            )
            return carry

        lax.fori_loop(0, NZ - 1, one, 0)
        sent.append((there.at[h], ar_send, (s, h, 1)))

    def sum_gather(s, h):
        _, _, own, _, there, result, _ = set_of(s)
        tall = own.shape[2]
        wait_for(there.at[h], ar_recv, (s, h, 1))
        total = own[h, z]
        for k in range(NZ - 1):
            total = total + there[h, k].astype(F32)
        row = pl.multiple_of(h * 4 * tall + (z // 2) * tall, 16)
        col = pl.multiple_of(c * 256 + lax.rem(z, 2) * 128, 128)
        mine = result.at[pl.ds(row, tall), pl.ds(col, 128)]
        mine[...] = total.astype(BF)

        def one(i, carry):
            d = lax.rem(i + 3, NZ - 1) + 1
            start(mine, mine, ar_send.at[s, h, 2], ar_recv.at[s, h, 2], at_z(d))
            return carry

        lax.fori_loop(0, NZ - 1, one, 0)
        sent.append((there.at[h], ar_send, (s, h, 2)))

    def half_of(s, h):
        _, _, own, _, _, result, _ = set_of(s)
        tall = own.shape[2]
        col = pl.multiple_of(c * 256, 128)
        return result.at[pl.ds(h * 4 * tall, 4 * tall), pl.ds(col, 256)]

    def sum_share(s, h):
        there = set_of(s)[4]
        wait_for(there.at[h], ar_recv, (s, h, 2))
        part = half_of(s, h)
        send(part, part, ar, (s, h, 3), sibling)

    def sum_end(s, h):
        wait_for(half_of(s, h), ar_recv, (s, h, 3))

    def piece(a, half, t, part):
        return gr[a].at[part, t, 0] if half == 0 else gr[a].at[t, part, 1]

    def add_blocks(out, first, terms, count):
        def one(k, carry):
            total = first(k)[...].astype(F32)
            for term in terms:
                total = total + term(k)[...].astype(F32)
            out(k)[...] = total.astype(BF)
            return carry

        lax.fori_loop(0, count, one, 0)

    def scatter_one(a):
        for half in range(2):
            _, m, _, go = places(half)
            right, far, left = around(m)
            send(piece(a, half, far, low), ra[a].at[half, 0, low], rs, (a, 0, half, 0), go(1))
            send(piece(a, half, far, high), ra[a].at[half, 0, high], rs, (a, 0, half, 1), go(3))
            send(piece(a, half, right, high), ra[a].at[half, 1, high], rs, (a, 1, half, 0), go(1))
            send(piece(a, half, left, low), ra[a].at[half, 1, low], rs, (a, 1, half, 1), go(3))

    def scatter_mid(a):
        for half in range(2):
            _, m, _, go = places(half)
            right, _, left = around(m)
            for side, (part, base, to, d) in enumerate(((low, 0, right, 1), (high, 2, left, 3))):
                wait_for(ra[a].at[half, 0, part], rs_recv, (a, 0, half, side))
                add_blocks(
                    lambda k: cb[a].at[half, base + k],
                    lambda k: piece(a, half, to, base + k),
                    (lambda k: ra[a].at[half, 0, base + k],),
                    2,
                )
                send(cb[a].at[half, part], ra[a].at[half, 2, part], rs, (a, 2, half, side), go(d))

    def scatter_two(a):
        for half in range(2):
            q, m, go, _ = places(half)
            wait_for(ra[a].at[half, 1, high], rs_recv, (a, 1, half, 0))
            wait_for(ra[a].at[half, 1, low], rs_recv, (a, 1, half, 1))
            wait_for(ra[a].at[half, 2, low], rs_recv, (a, 2, half, 0))
            wait_for(ra[a].at[half, 2, high], rs_recv, (a, 2, half, 1))
            add_blocks(
                lambda k: rb[a].at[half, k],
                lambda k: piece(a, half, m, k),
                (lambda k: ra[a].at[half, 1, k], lambda k: ra[a].at[half, 2, k]),
                4,
            )
            for d in (2, 1, 3):
                send(
                    rb[a].at[half, lax.rem(q + d, 4)], rc[a].at[half, d - 1],
                    rs, (a, 3, half, d - 1), go(d),
                )

    def scatter_end(a):
        squares = jnp.zeros((8, 128), F32)
        for half in range(2):
            q, _, _, _ = places(half)
            total = rb[a][half, q].astype(F32)
            for d in range(3):
                wait_for(rc[a].at[half, d], rs_recv, (a, 3, half, d))
                total = total + rc[a][half, d].astype(F32)
            gouts[a][half * 16 : (half + 1) * 16, :] = total
            sq = total * total
            sq = sq[0:8] + sq[8:16]
            for j in range(cols[a] // 128):
                squares = squares + sq[:, j * 128 : (j + 1) * 128]
        return squares

    def gradient(a, left, right):
        ranks_t[...] = left[...].T
        step = 768 if cols[a] % 768 == 0 else 384

        def one(j, carry):
            at = pl.ds(pl.multiple_of(j * step, 128), step)
            tile = dot_nn(ranks_t[...], right[:, at]).astype(BF)
            gr[a][:, :, :, :, at] = tile.reshape(NX, NY, 2, 16, step)
            return carry

        lax.fori_loop(0, cols[a] // step, one, 0)

    def tile_of(a, at, n):
        return w[a][:, :, :, :, at].reshape(RANK, n)

    def rows_of(h):
        return pl.ds(h * HALF, HALF)

    def stage_zero(h):
        sum_send(0, h, tok[rows_of(h), :], PI)

    def stage_one(h):
        left = rank[0, rows_of(h), :]

        def one(j, carry):
            at = pl.ds(pl.multiple_of(j * 768, 128), 768)
            pre = jnp.maximum(dot_nn(left, tile_of(PO, at, 768)), 0.0)
            relu[rows_of(h), at] = pre
            hid[rows_of(h), at] = (pre * pre).astype(BF)
            return carry

        lax.fori_loop(0, cols[PO] // 768, one, 0)

    def stage_two(h):
        left = rank[1, rows_of(h), :]

        def one(j, carry):
            at = pl.ds(pl.multiple_of(j * 384, 128), 384)
            misfit = dot_nn(left, tile_of(QO, at, 384)) - tgt[rows_of(h), at].astype(F32)
            gout[rows_of(h), at] = (misfit * (1.0 / TOTAL)).astype(BF)
            sq = (misfit * misfit).reshape(HALF // 8, 8, 384).sum(axis=0)
            loss_acc[...] += sq[:, 0:128] + sq[:, 128:256] + sq[:, 256:384]
            return carry

        lax.fori_loop(0, cols[QO] // 384, one, 0)

    def stage_back(h):
        up = dot_nn(rank[1, rows_of(h), :], gram[...]) - rank[2, rows_of(h), :].astype(F32)
        back[rows_of(h), :] = (up * (1.0 / TOTAL)).astype(BF)

    def stage_three(h):
        left = back[rows_of(h), :]

        def one(j, carry):
            at = pl.ds(pl.multiple_of(j * 768, 128), 768)
            up = dot_nn(left, tile_of(QI, at, 768))
            gpre[rows_of(h), at] = (up * 2.0 * relu[rows_of(h), at]).astype(BF)
            return carry

        lax.fori_loop(0, cols[QI] // 768, one, 0)

    def gram_send(h):
        sum_send(GRAM, h, w[QO][2 * h : 2 * h + 2].reshape(256, cols[QO]), QO)

    loss_acc[...] = jnp.zeros_like(loss_acc)
    loads[0].wait()
    cast(PI)
    pl.semaphore_wait(barrier, 2 * (DP - 1))
    gather_one(PI)
    loads[4].wait()
    cast(QO)
    gather_one(QO)
    loads[1].wait()
    cast(PO)
    gather_two(PI)
    gather_two(QO)
    gather_one(PO)
    loads[3].wait()
    cast(QI)
    gather_last(PI)
    gather_last(QO)
    gather_two(PO)
    gather_one(QI)
    loads[2].wait()
    loads[5].wait()
    gather_end(PI)
    stage_zero(0)
    sum_scatter(0, 0)
    stage_zero(1)
    sum_scatter(0, 1)
    gather_end(QO)
    sum_send(2, 0, tgt[rows_of(0), :], QO)
    sum_scatter(2, 0)
    sum_send(2, 1, tgt[rows_of(1), :], QO)
    sum_scatter(2, 1)
    sum_gather(0, 0)
    sum_gather(0, 1)
    gather_last(PO)
    gather_two(QI)
    gram_send(0)
    sum_scatter(GRAM, 0)
    gram_send(1)
    sum_scatter(GRAM, 1)
    sum_share(0, 0)
    sum_share(0, 1)
    gather_last(QI)
    sum_gather(2, 0)
    sum_gather(2, 1)
    gather_end(PO)
    sum_end(0, 0)
    stage_one(0)
    sum_end(0, 1)
    stage_one(1)
    sum_gather(GRAM, 0)
    sum_gather(GRAM, 1)
    sum_share(2, 0)
    sum_share(2, 1)
    gather_end(QI)
    sum_send(1, 0, hid[rows_of(0), :], QI)
    sum_scatter(1, 0)
    sum_send(1, 1, hid[rows_of(1), :], QI)
    sum_scatter(1, 1)
    sum_share(GRAM, 0)
    sum_share(GRAM, 1)
    sum_gather(1, 0)
    sum_gather(1, 1)
    sum_end(2, 0)
    sum_end(2, 1)
    sum_end(GRAM, 0)
    sum_end(GRAM, 1)
    sum_share(1, 0)
    sum_end(1, 0)
    stage_two(0)
    stage_back(0)
    sum_share(1, 1)
    sum_end(1, 1)
    stage_two(1)
    gradient(QO, rank.at[1], gout)
    scatter_one(QO)
    stage_back(1)
    gradient(QI, back, hid)
    scatter_one(QI)
    stage_three(0)
    sum_send(3, 0, gpre[rows_of(0), :], PO)
    sum_scatter(3, 0)
    stage_three(1)
    sum_send(3, 1, gpre[rows_of(1), :], PO)
    sum_scatter(3, 1)
    scatter_mid(QO)
    gradient(PO, rank.at[0], gpre)
    scatter_one(PO)
    sum_gather(3, 0)
    sum_gather(3, 1)
    scatter_mid(QI)
    sum_share(3, 0)
    sum_share(3, 1)
    scatter_two(QO)
    sum_end(3, 0)
    sum_end(3, 1)
    gradient(PI, rank.at[3], tok)
    scatter_one(PI)
    scatter_mid(PO)
    scatter_two(QI)
    squares = scatter_end(QO)
    scatter_mid(PI)
    scatter_two(PO)
    scatter_two(PI)
    squares = squares + scatter_end(QI)
    squares = squares + scatter_end(PO)
    squares = squares + scatter_end(PI)

    sc_buf[0, me_t, 0] = squares
    sc_buf[0, me_t, 1] = loss_acc[...]

    def over_tensor(k, carry):
        own = sc_buf.at[0, me_t]
        start(own, own, sc_send.at[0], sc_recv.at[0], (me_dp, lax.rem(me_t + k, TP)))
        return carry

    lax.fori_loop(1, TP, over_tensor, 0)
    wait_for(sc_buf.at[0, pl.ds(0, TP - 1)], sc_recv, (0,))
    sc_buf[1, me_dp] = jnp.sum(sc_buf[0], axis=0)

    def over_dp(k, carry):
        own = sc_buf.at[1, me_dp]
        start(own, own, sc_send.at[1], sc_recv.at[1], (lax.rem(me_dp + k, DP), me_t))
        return carry

    lax.fori_loop(1, DP, over_dp, 0)
    wait_for(sc_buf.at[1, pl.ds(0, DP - 1)], sc_recv, (1,))
    stat[...] = jnp.sum(sc_buf[1], axis=0)

    for ref, sem, spot_of in sent:
        wait_for(ref, sem, spot_of)
    for k in range(2):
        wait_for(sc_buf.at[k, pl.ds(0, TP - 1)], sc_send, (k,))


def adam_body(
    stat, g_pi, g_po, g_qi, g_qo, p_pi, p_po, p_qi, p_qo, wm, ws, hm, hs,
    n_pi, n_po, n_qi, n_qo, nwm, nws, nhm, nhs, loss,
    ga, gb, gc, gd, pa, pb, pc, pd, ma, mb, mc, md, va, vb, vc, vd, in_sem, out_sem,
):
    jobs = (
        (g_pi, p_pi, wm, ws, 0, n_pi, nwm, nws, ga, pa, ma, va),
        (g_qo, p_qo, wm, ws, 1, n_qo, nwm, nws, gd, pd, md, vd),
        (g_po, p_po, hm, hs, 0, n_po, nhm, nhs, gb, pb, mb, vb),
        (g_qi, p_qi, hm, hs, 1, n_qi, nhm, nhs, gc, pc, mc, vc),
    )
    ins, outs = [], []
    for j, (g, p, m, v, k, _, _, _, gs, ps, ms, vs) in enumerate(jobs):
        ins.append([
            pltpu.make_async_copy(src, dst, in_sem.at[j, i])
            for i, (src, dst) in enumerate(((g, gs), (p, ps), (m.at[k], ms), (v.at[k], vs)))
        ])
        for cp in ins[j]:
            cp.start()
    squares = jnp.sum(stat[0])
    scale = 1.0 / jnp.maximum(jnp.sqrt(squares), 1.0)
    loss[0, 0] = jnp.sum(stat[1]) / (2.0 * TOTAL)
    for j, (_, _, _, _, k, new_p, new_m, new_v, gs, ps, ms, vs) in enumerate(jobs):
        for cp in ins[j]:
            cp.wait()
        grad = gs[...] * scale
        mean = beta_one * ms[...] + (1.0 - beta_one) * grad
        square = beta_two * vs[...] + (1.0 - beta_two) * grad * grad
        corrected = mean * (1.0 / (1.0 - beta_one**10))
        spread = jnp.sqrt(square * (1.0 / (1.0 - beta_two**10))) + tiny_eps
        ps[...] = ps[...] - learn_rate * corrected / spread
        ms[...] = mean
        vs[...] = square
        for i, (src, dst) in enumerate(((ps, new_p), (ms, new_m.at[k]), (vs, new_v.at[k]))):
            cp = pltpu.make_async_copy(src, dst, out_sem.at[j, i])
            cp.start()
            outs.append(cp)
    for cp in outs:
        cp.wait()


def shards(
    tokens, target, first_in, first_out, second_in, second_out,
    width_mean, width_square, hidden_mean, hidden_square,
):
    wide = first_in.shape[1]
    deep = first_out.shape[1]
    cols = (wide, deep, deep, wide)
    vm = pltpu.VMEM
    dma = pltpu.SemaphoreType.DMA
    scratch = [vm((TOKD, wide), BF), vm((TOKD, wide), BF)]
    scratch += [vm((ROWS, n), F32) for n in cols]
    scratch += [vm((NX, NY, 2, 16, n), BF) for n in cols]
    scratch += [vm((NX, NY, 2, 16, n), BF) for n in cols]
    scratch += [vm((2, 3, 4, 16, n), BF) for n in cols]
    scratch += [vm((2, 4, 16, n), BF) for n in cols]
    scratch += [vm((2, 3, 16, n), BF) for n in cols]
    scratch += [vm((2, 4, 16, n), BF) for n in cols]
    scratch += [
        vm((4, TOKD, RANK), BF),
        vm((TOKD, RANK), BF),
        vm((RANK, TOKD), BF),
        vm((TOKD, deep), F32),
        vm((TOKD, deep), BF),
        vm((TOKD, deep), BF),
        vm((TOKD, wide), BF),
        vm((2, HALF, 256), F32),
        vm((4, 2, HALF, 256), BF),
        vm((4, 2, HALF, 256), BF),
        vm((4, 2, NZ, 48, 128), F32),
        vm((4, 2, NZ, 48, 128), BF),
        vm((4, 2, NZ - 1, 48, 128), BF),
        vm((RANK, RANK), BF),
        vm((2, 256, 256), F32),
        vm((2, 256, 256), BF),
        vm((2, 256, 256), BF),
        vm((2, NZ, 64, 128), F32),
        vm((2, NZ, 64, 128), BF),
        vm((2, NZ - 1, 64, 128), BF),
        vm((8, 128), F32),
        vm((2, 16, 2, 8, 128), F32),
        dma((6,)),
        dma((4, 3, 2, 3)), dma((4, 3, 2, 3)),
        dma((4, 4, 2, 3)), dma((4, 4, 2, 3)),
        dma((5, 2, 4)), dma((5, 2, 4)),
        dma((2,)), dma((2,)),
    ]
    whole = pl.BlockSpec(memory_space=pltpu.VMEM)
    g_pi, g_po, g_qi, g_qo, stat = pl.pallas_call(
        body,
        name="step",
        out_shape=[jax.ShapeDtypeStruct((ROWS, n), F32) for n in cols]
        + [jax.ShapeDtypeStruct((2, 8, 128), F32)],
        in_specs=[pl.BlockSpec(memory_space=pl.ANY)] * 6,
        out_specs=[whole] * 5,
        scratch_shapes=scratch,
        compiler_params=pltpu.CompilerParams(
            collective_id=0, has_side_effects=True, vmem_limit_bytes=58 * 2**20
        ),
    )(tokens, target, first_in, first_out, second_in, second_out)

    anywhere = pl.BlockSpec(memory_space=pl.ANY)
    outs = pl.pallas_call(
        adam_body,
        name="adam",
        out_shape=[jax.ShapeDtypeStruct((ROWS, n), F32) for n in cols]
        + [jax.ShapeDtypeStruct((2, ROWS, n), F32) for n in (wide, wide, deep, deep)]
        + [jax.ShapeDtypeStruct((1, 1), F32)],
        in_specs=[whole] + [anywhere] * 12,
        out_specs=[anywhere] * 8 + [pl.BlockSpec(memory_space=pltpu.SMEM)],
        scratch_shapes=[vm((ROWS, n), F32) for n in cols] * 4 + [dma((4, 4)), dma((4, 3))],
        compiler_params=pltpu.CompilerParams(vmem_limit_bytes=60 * 2**20),
    )(
        stat, g_pi, g_po, g_qi, g_qo, first_in, first_out, second_in, second_out,
        width_mean, width_square, hidden_mean, hidden_square,
    )
    return tuple(outs[:8]) + (outs[8].reshape(()),)


def solution(mesh):
    two = P("dp", "tensor")
    three = P(None, "dp", "tensor")
    return jax.shard_map(
        shards,
        mesh=mesh,
        in_specs=(two,) * 6 + (three,) * 4,
        out_specs=(two,) * 4 + (three,) * 4 + (P(),),
        check_vma=False,
    )
```

time: 159 us -> 140 us (0.88)
  Pallas kernels: 154 us -> 139 us
  local copies, waits for them, and re-layouts: 4.38 us -> 0 us
    pallas_call x1, Pallas kernels: 151 us -> 135 us  [shards(): pl.pallas_call(body, name='step', out_shape=[jax.ShapeDtypeStruct((ROWS,...]
    unnamed x26 -> x0, local copies, waits for them, and re-layouts: 4.38 us -> none
    pallas_call x1, Pallas kernels: 2.74 us -> 4.68 us  [shards(): pl.pallas_call(adam_body, name='adam', out_shape=[jax.ShapeDtypeStruct((R...]
where the time goes in v2:
time: 140 us
  Pallas kernels  139 us (99%)
    pallas_call x1, Pallas kernels, shards(): pl.pallas_call(body, name='step', out_shape=[jax.ShapeDtypeStruct((ROWS,...  135 us
    pallas_call x1, Pallas kernels, shards(): pl.pallas_call(adam_body, name='adam', out_shape=[jax.ShapeDtypeStruct((R...  4.68 us

profile of v2, /device:TPU:1, one launch (start us, length us, event | category | flops | bytes accessed | tf_op | source)
XLA Modules:
  0.0 139.8 jit_solution(1335954759561330155)
XLA Ops:
  0.6 134.5 %step.1 = (f32[32,1152]{1,0:T(8,128)}, f32[32,2304]{1,0:T(8,128)}, f32[32,2304]{1,0:T(8,128)}, f32[32,1152]{1,0:T(8,128)}, f32[2,8,128]{2,1,0:T(8,128)}) custom-call(bf16[384,1152]{1,0:T(8,128)(2,1)} %tokens.1, bf16[384,1152]{1,0:T(8,128)(2,1)} %target.1, f32[32,1152]{1,0:T(8,128)} %p_pi.1, f32[32,2304]{1,0:T(8,128)} %p_po.1, f32[32,2304]{1,0:T(8,128)} %p_qi.1, ...), custom_call_target="tpu_custom_call" | custom-call | tf_op jit(solution)/shard_map/step/pallas_call | solution.py:596
  135.2 4.7 %adam.1 = (f32[32,1152]{1,0:T(8,128)}, f32[32,2304]{1,0:T(8,128)}, f32[32,2304]{1,0:T(8,128)}, f32[32,1152]{1,0:T(8,128)}, f32[2,32,1152]{2,1,0:T(8,128)}, /*ind...) custom-call(f32[2,8,128]{2,1,0:T(8,128)} %get-tuple-element.23.stat, ...), custom_call_target="tpu_custom_call" | custom-call | tf_op jit(solution)/shard_map/adam/pallas_call | solution.py:610

commit v3 on v2

--- a/solution.py
+++ b/solution.py
@@ -44,11 +44,11 @@
     tok, tgt, wf0, wf1, wf2, wf3,
     w0, w1, w2, w3, gr0, gr1, gr2, gr3,
     ra0, ra1, ra2, ra3, rb0, rb1, rb2, rb3, rc0, rc1, rc2, rc3,
-    cb0, cb1, cb2, cb3,
+    cb0, cb1, cb2, cb3, cc0, cc1, cc2, cc3,
     rank, back, ranks_t, relu, hid, gpre, gout, partial,
     sib_send, sib_recv, z_keep, z_send, z_recv,
     gram, gpartial, gsib_send, gsib_recv, gz_keep, gz_send, gz_recv, loss_acc, sc_buf,
-    ld_sem, ag_send, ag_recv, rs_send, rs_recv, ar_send, ar_recv, sc_send, sc_recv,
+    ld_sem, ag_send, ag_recv, rs_send, rs_recv, ar_send, ar_recv, gr_send, gr_recv, sc_send, sc_recv,
 ):
     me_dp = lax.axis_index("dp")
     me_t = lax.axis_index("tensor")
@@ -61,6 +61,7 @@
     rb = (rb0, rb1, rb2, rb3)
     rc = (rc0, rc1, rc2, rc3)
     cb = (cb0, cb1, cb2, cb3)
+    cc = (cc0, cc1, cc2, cc3)
     gouts = (g_pi, g_po, g_qi, g_qo)
     cols = tuple(r.shape[-1] for r in wf)
 
@@ -96,8 +97,25 @@
     ar = (ar_send, ar_recv)
     low, high = pl.ds(0, 2), pl.ds(2, 2)
 
+    def cut(a):
+        n = cols[a] // 256 * 128
+        return pl.ds(0, n), pl.ds(n, cols[a] - n)
+
     def around(m):
         return lax.rem(m + 1, 4), lax.rem(m + 2, 4), lax.rem(m + 3, 4)
+
+    barrier = pltpu.get_barrier_semaphore()
+
+    def greet(k, carry):
+        pl.semaphore_signal(
+            barrier, inc=1, device_id=(lax.rem(me_dp + k, DP), me_t), device_id_type=MESH
+        )
+        pl.semaphore_signal(
+            barrier, inc=1, device_id=(me_dp, lax.rem(me_t + k, TP)), device_id_type=MESH
+        )
+        return carry
+
+    lax.fori_loop(1, DP, greet, 0, unroll=True)
 
     loads = [
         pltpu.make_async_copy(s, d, ld_sem.at[k])
@@ -108,19 +126,6 @@
     for cp in loads:
         cp.start()
 
-    barrier = pltpu.get_barrier_semaphore()
-
-    def greet(k, carry):
-        pl.semaphore_signal(
-            barrier, inc=1, device_id=(lax.rem(me_dp + k, DP), me_t), device_id_type=MESH
-        )
-        pl.semaphore_signal(
-            barrier, inc=1, device_id=(me_dp, lax.rem(me_t + k, TP)), device_id_type=MESH
-        )
-        return carry
-
-    lax.fori_loop(1, DP, greet, 0)
-
     def cast(a):
         w[a][x, y] = wf[a][...].astype(BF).reshape(2, 16, cols[a])
 
@@ -147,6 +152,21 @@
             row = slot(a, half, pl.ds(0, 4), q)
             send(row, row, ag, (a, 1, half, 0), go(1))
             send(row, row, ag, (a, 1, half, 1), go(3))
+
+    def gather_all(a):
+        for half in range(2):
+            m, q, _, go = places(half)
+            for d in range(3):
+                wait_for(slot(a, half, m, q), ag_recv, (a, 0, half, d))
+            row = slot(a, half, pl.ds(0, 4), q)
+            for d in (2, 1, 3):
+                send(row, row, ag, (a, 1, half, d - 1), go(d))
+
+    def gather_done(a):
+        for half in range(2):
+            _, q, _, _ = places(half)
+            for d in range(3):
+                wait_for(slot(a, half, pl.ds(0, 4), q), ag_recv, (a, 1, half, d))
 
     def gather_last(a):
         for half in range(2):
@@ -166,9 +186,11 @@
             wait_for(slot(a, half, low, far), ag_recv, (a, 2, half, 0))
             wait_for(slot(a, half, high, far), ag_recv, (a, 2, half, 1))
 
+    gram_rows = pl.ds(pl.multiple_of(x * 128, 128), 128)
+
     def set_of(s):
         if s == GRAM:
-            return gsib_send, gsib_recv, gz_keep, gz_send, gz_recv, gram, gpartial
+            return gsib_send, gsib_recv, gz_keep, gz_send, gz_recv, gram.at[gram_rows], gpartial
         return (
             sib_send.at[s], sib_recv.at[s], z_keep.at[s], z_send.at[s], z_recv.at[s], rank.at[s], partial,
         )
@@ -199,7 +221,7 @@
             )
             return carry
 
-        lax.fori_loop(0, NZ - 1, one, 0)
+        lax.fori_loop(0, NZ - 1, one, 0, unroll=True)
         sent.append((there.at[h], ar_send, (s, h, 1)))
 
     def sum_gather(s, h):
@@ -219,7 +241,7 @@
             start(mine, mine, ar_send.at[s, h, 2], ar_recv.at[s, h, 2], at_z(d))
             return carry
 
-        lax.fori_loop(0, NZ - 1, one, 0)
+        lax.fori_loop(0, NZ - 1, one, 0, unroll=True)
         sent.append((there.at[h], ar_send, (s, h, 2)))
 
     def half_of(s, h):
@@ -292,6 +314,63 @@
                     rs, (a, 3, half, d - 1), go(d),
                 )
 
+    def scatter_near(a):
+        left_cols, right_cols = cut(a)
+        for half in range(2):
+            q, m, go, _ = places(half)
+            wait_for(ra[a].at[half, 1, high], rs_recv, (a, 1, half, 0))
+            wait_for(ra[a].at[half, 1, low], rs_recv, (a, 1, half, 1))
+            wait_for(ra[a].at[half, 2, low], rs_recv, (a, 2, half, 0))
+            wait_for(ra[a].at[half, 2, high], rs_recv, (a, 2, half, 1))
+            add_blocks(
+                lambda k: rb[a].at[half, k],
+                lambda k: piece(a, half, m, k),
+                (lambda k: ra[a].at[half, 1, k], lambda k: ra[a].at[half, 2, k]),
+                4,
+            )
+            right, far, left = around(q)
+            for kind, side, owner, part, d in (
+                (0, 0, far, left_cols, 1),
+                (0, 1, far, right_cols, 3),
+                (1, 0, right, right_cols, 1),
+                (1, 1, left, left_cols, 3),
+            ):
+                send(
+                    rb[a].at[half, owner, :, part], rc[a].at[half, kind, :, part],
+                    rs, (a, 3 + kind, half, side), go(d),
+                )
+
+    def scatter_late(a):
+        left_cols, right_cols = cut(a)
+        for half in range(2):
+            q, _, go, _ = places(half)
+            right, _, left = around(q)
+            for side, (part, owner, d) in enumerate(((left_cols, right, 1), (right_cols, left, 3))):
+                wait_for(rc[a].at[half, 0, :, part], rs_recv, (a, 3, half, side))
+                total = rb[a][half, owner, :, part].astype(F32) + rc[a][half, 0, :, part].astype(F32)
+                cc[a][half, :, part] = total.astype(BF)
+                send(
+                    cc[a].at[half, :, part], rc[a].at[half, 2, :, part],
+                    rs, (a, 5, half, side), go(d),
+                )
+
+    def scatter_done(a):
+        left_cols, right_cols = cut(a)
+        squares = jnp.zeros((8, 128), F32)
+        for half in range(2):
+            q, _, _, _ = places(half)
+            wait_for(rc[a].at[half, 1, :, right_cols], rs_recv, (a, 4, half, 0))
+            wait_for(rc[a].at[half, 1, :, left_cols], rs_recv, (a, 4, half, 1))
+            wait_for(rc[a].at[half, 2, :, left_cols], rs_recv, (a, 5, half, 0))
+            wait_for(rc[a].at[half, 2, :, right_cols], rs_recv, (a, 5, half, 1))
+            total = rb[a][half, q].astype(F32) + rc[a][half, 1].astype(F32) + rc[a][half, 2].astype(F32)
+            gouts[a][half * 16 : (half + 1) * 16, :] = total
+            sq = total * total
+            sq = sq[0:8] + sq[8:16]
+            for j in range(cols[a] // 128):
+                squares = squares + sq[:, j * 128 : (j + 1) * 128]
+        return squares
+
     def scatter_end(a):
         squares = jnp.zeros((8, 128), F32)
         for half in range(2):
@@ -368,8 +447,17 @@
 
         lax.fori_loop(0, cols[QI] // 768, one, 0)
 
-    def gram_send(h):
-        sum_send(GRAM, h, w[QO][2 * h : 2 * h + 2].reshape(256, cols[QO]), QO)
+    def gram_send():
+        sum_send(GRAM, 0, w[QO][x].reshape(128, cols[QO]), QO)
+
+    def gram_spread():
+        part = gram.at[gram_rows]
+        for d in (2, 1, 3):
+            send(part, part, (gr_send, gr_recv), (d - 1,), at_x(d))
+
+    def gram_end():
+        for d in range(3):
+            wait_for(gram.at[gram_rows], gr_recv, (d,))
 
     loss_acc[...] = jnp.zeros_like(loss_acc)
     loads[0].wait()
@@ -397,46 +485,42 @@
     sum_scatter(0, 0)
     stage_zero(1)
     sum_scatter(0, 1)
+    sum_gather(0, 0)
+    sum_gather(0, 1)
+    gather_last(PO)
+    gather_all(QI)
     gather_end(QO)
+    gram_send()
+    sum_scatter(GRAM, 0)
     sum_send(2, 0, tgt[rows_of(0), :], QO)
     sum_scatter(2, 0)
     sum_send(2, 1, tgt[rows_of(1), :], QO)
     sum_scatter(2, 1)
-    sum_gather(0, 0)
-    sum_gather(0, 1)
-    gather_last(PO)
-    gather_two(QI)
-    gram_send(0)
-    sum_scatter(GRAM, 0)
-    gram_send(1)
-    sum_scatter(GRAM, 1)
     sum_share(0, 0)
     sum_share(0, 1)
-    gather_last(QI)
     sum_gather(2, 0)
     sum_gather(2, 1)
+    sum_gather(GRAM, 0)
     gather_end(PO)
     sum_end(0, 0)
     stage_one(0)
     sum_end(0, 1)
     stage_one(1)
-    sum_gather(GRAM, 0)
-    sum_gather(GRAM, 1)
     sum_share(2, 0)
     sum_share(2, 1)
-    gather_end(QI)
+    sum_share(GRAM, 0)
+    gather_done(QI)
     sum_send(1, 0, hid[rows_of(0), :], QI)
     sum_scatter(1, 0)
     sum_send(1, 1, hid[rows_of(1), :], QI)
     sum_scatter(1, 1)
-    sum_share(GRAM, 0)
-    sum_share(GRAM, 1)
+    sum_end(GRAM, 0)
+    gram_spread()
     sum_gather(1, 0)
     sum_gather(1, 1)
     sum_end(2, 0)
     sum_end(2, 1)
-    sum_end(GRAM, 0)
-    sum_end(GRAM, 1)
+    gram_end()
     sum_share(1, 0)
     sum_end(1, 0)
     stage_two(0)
@@ -463,19 +547,22 @@
     scatter_mid(QI)
     sum_share(3, 0)
     sum_share(3, 1)
-    scatter_two(QO)
+    scatter_near(QO)
     sum_end(3, 0)
     sum_end(3, 1)
     gradient(PI, rank.at[3], tok)
     scatter_one(PI)
+    scatter_late(QO)
     scatter_mid(PO)
-    scatter_two(QI)
-    squares = scatter_end(QO)
+    scatter_near(QI)
     scatter_mid(PI)
-    scatter_two(PO)
+    scatter_near(PO)
+    scatter_late(QI)
+    squares = scatter_done(QO)
     scatter_two(PI)
-    squares = squares + scatter_end(QI)
-    squares = squares + scatter_end(PO)
+    scatter_late(PO)
+    squares = squares + scatter_done(QI)
+    squares = squares + scatter_done(PO)
     squares = squares + scatter_end(PI)
 
     sc_buf[0, me_t, 0] = squares
@@ -486,7 +573,7 @@
         start(own, own, sc_send.at[0], sc_recv.at[0], (me_dp, lax.rem(me_t + k, TP)))
         return carry
 
-    lax.fori_loop(1, TP, over_tensor, 0)
+    lax.fori_loop(1, TP, over_tensor, 0, unroll=True)
     wait_for(sc_buf.at[0, pl.ds(0, TP - 1)], sc_recv, (0,))
     sc_buf[1, me_dp] = jnp.sum(sc_buf[0], axis=0)
 
@@ -495,7 +582,7 @@
         start(own, own, sc_send.at[1], sc_recv.at[1], (lax.rem(me_dp + k, DP), me_t))
         return carry
 
-    lax.fori_loop(1, DP, over_dp, 0)
+    lax.fori_loop(1, DP, over_dp, 0, unroll=True)
     wait_for(sc_buf.at[1, pl.ds(0, DP - 1)], sc_recv, (1,))
     stat[...] = jnp.sum(sc_buf[1], axis=0)
 
@@ -508,42 +595,24 @@
 def adam_body(
     stat, g_pi, g_po, g_qi, g_qo, p_pi, p_po, p_qi, p_qo, wm, ws, hm, hs,
     n_pi, n_po, n_qi, n_qo, nwm, nws, nhm, nhs, loss,
-    ga, gb, gc, gd, pa, pb, pc, pd, ma, mb, mc, md, va, vb, vc, vd, in_sem, out_sem,
 ):
-    jobs = (
-        (g_pi, p_pi, wm, ws, 0, n_pi, nwm, nws, ga, pa, ma, va),
-        (g_qo, p_qo, wm, ws, 1, n_qo, nwm, nws, gd, pd, md, vd),
-        (g_po, p_po, hm, hs, 0, n_po, nhm, nhs, gb, pb, mb, vb),
-        (g_qi, p_qi, hm, hs, 1, n_qi, nhm, nhs, gc, pc, mc, vc),
-    )
-    ins, outs = [], []
-    for j, (g, p, m, v, k, _, _, _, gs, ps, ms, vs) in enumerate(jobs):
-        ins.append([
-            pltpu.make_async_copy(src, dst, in_sem.at[j, i])
-            for i, (src, dst) in enumerate(((g, gs), (p, ps), (m.at[k], ms), (v.at[k], vs)))
-        ])
-        for cp in ins[j]:
-            cp.start()
     squares = jnp.sum(stat[0])
     scale = 1.0 / jnp.maximum(jnp.sqrt(squares), 1.0)
     loss[0, 0] = jnp.sum(stat[1]) / (2.0 * TOTAL)
-    for j, (_, _, _, _, k, new_p, new_m, new_v, gs, ps, ms, vs) in enumerate(jobs):
-        for cp in ins[j]:
-            cp.wait()
-        grad = gs[...] * scale
-        mean = beta_one * ms[...] + (1.0 - beta_one) * grad
-        square = beta_two * vs[...] + (1.0 - beta_two) * grad * grad
+    for g, p, m, v, k, new_p, new_m, new_v in (
+        (g_pi, p_pi, wm, ws, 0, n_pi, nwm, nws),
+        (g_qo, p_qo, wm, ws, 1, n_qo, nwm, nws),
+        (g_po, p_po, hm, hs, 0, n_po, nhm, nhs),
+        (g_qi, p_qi, hm, hs, 1, n_qi, nhm, nhs),
+    ):
+        grad = g[...] * scale
+        mean = beta_one * m[k] + (1.0 - beta_one) * grad
+        square = beta_two * v[k] + (1.0 - beta_two) * grad * grad
         corrected = mean * (1.0 / (1.0 - beta_one**10))
         spread = jnp.sqrt(square * (1.0 / (1.0 - beta_two**10))) + tiny_eps
-        ps[...] = ps[...] - learn_rate * corrected / spread
-        ms[...] = mean
-        vs[...] = square
-        for i, (src, dst) in enumerate(((ps, new_p), (ms, new_m.at[k]), (vs, new_v.at[k]))):
-            cp = pltpu.make_async_copy(src, dst, out_sem.at[j, i])
-            cp.start()
-            outs.append(cp)
-    for cp in outs:
-        cp.wait()
+        new_p[...] = p[...] - learn_rate * corrected / spread
+        new_m[k] = mean
+        new_v[k] = square
 
 
 def shards(
@@ -563,6 +632,7 @@
     scratch += [vm((2, 4, 16, n), BF) for n in cols]
     scratch += [vm((2, 3, 16, n), BF) for n in cols]
     scratch += [vm((2, 4, 16, n), BF) for n in cols]
+    scratch += [vm((2, 16, n), BF) for n in cols]
     scratch += [
         vm((4, TOKD, RANK), BF),
         vm((TOKD, RANK), BF),
@@ -578,18 +648,19 @@
         vm((4, 2, NZ, 48, 128), BF),
         vm((4, 2, NZ - 1, 48, 128), BF),
         vm((RANK, RANK), BF),
-        vm((2, 256, 256), F32),
-        vm((2, 256, 256), BF),
-        vm((2, 256, 256), BF),
-        vm((2, NZ, 64, 128), F32),
-        vm((2, NZ, 64, 128), BF),
-        vm((2, NZ - 1, 64, 128), BF),
+        vm((1, 128, 256), F32),
+        vm((1, 128, 256), BF),
+        vm((1, 128, 256), BF),
+        vm((1, NZ, 32, 128), F32),
+        vm((1, NZ, 32, 128), BF),
+        vm((1, NZ - 1, 32, 128), BF),
         vm((8, 128), F32),
         vm((2, 16, 2, 8, 128), F32),
         dma((6,)),
         dma((4, 3, 2, 3)), dma((4, 3, 2, 3)),
-        dma((4, 4, 2, 3)), dma((4, 4, 2, 3)),
+        dma((4, 6, 2, 3)), dma((4, 6, 2, 3)),
         dma((5, 2, 4)), dma((5, 2, 4)),
+        dma((3,)), dma((3,)),
         dma((2,)), dma((2,)),
     ]
     whole = pl.BlockSpec(memory_space=pltpu.VMEM)
@@ -606,16 +677,14 @@
         ),
     )(tokens, target, first_in, first_out, second_in, second_out)
 
-    anywhere = pl.BlockSpec(memory_space=pl.ANY)
     outs = pl.pallas_call(
         adam_body,
         name="adam",
         out_shape=[jax.ShapeDtypeStruct((ROWS, n), F32) for n in cols]
         + [jax.ShapeDtypeStruct((2, ROWS, n), F32) for n in (wide, wide, deep, deep)]
         + [jax.ShapeDtypeStruct((1, 1), F32)],
-        in_specs=[whole] + [anywhere] * 12,
-        out_specs=[anywhere] * 8 + [pl.BlockSpec(memory_space=pltpu.SMEM)],
-        scratch_shapes=[vm((ROWS, n), F32) for n in cols] * 4 + [dma((4, 4)), dma((4, 3))],
+        in_specs=[whole] * 13,
+        out_specs=[whole] * 8 + [pl.BlockSpec(memory_space=pltpu.SMEM)],
         compiler_params=pltpu.CompilerParams(vmem_limit_bytes=60 * 2**20),
     )(
         stat, g_pi, g_po, g_qi, g_qo, first_in, first_out, second_in, second_out,

time: 140 us -> 135 us (0.964)
  Pallas kernels: 139 us -> 134 us
    pallas_call x1, Pallas kernels: 135 us -> 130 us  [shards(): pl.pallas_call(body, name='step', out_shape=[jax.ShapeDtypeStruct((ROWS,...]
where the time goes in v3:
time: 135 us
  Pallas kernels  134 us (99%)
    pallas_call x1, Pallas kernels, shards(): pl.pallas_call(body, name='step', out_shape=[jax.ShapeDtypeStruct((ROWS,...  130 us
    pallas_call x1, Pallas kernels, shards(): pl.pallas_call(adam_body, name='adam', out_shape=[jax.ShapeDtypeStruct((R...  4.26 us

profile of v3, /device:TPU:1, one launch (start us, length us, event | category | flops | bytes accessed | tf_op | source)
XLA Modules:
  0.0 135.3 jit_solution(818307682258152613)
XLA Ops:
  0.6 130.2 %step.1 = (f32[32,1152]{1,0:T(8,128)}, f32[32,2304]{1,0:T(8,128)}, f32[32,2304]{1,0:T(8,128)}, f32[32,1152]{1,0:T(8,128)}, f32[2,8,128]{2,1,0:T(8,128)}) custom-call(bf16[384,1152]{1,0:T(8,128)(2,1)} %tokens.1, bf16[384,1152]{1,0:T(8,128)(2,1)} %target.1, f32[32,1152]{1,0:T(8,128)} %p_pi.1, f32[32,2304]{1,0:T(8,128)} %p_po.1, f32[32,2304]{1,0:T(8,128)} %p_qi.1, ...), custom_call_target="tpu_custom_call" | custom-call | tf_op jit(solution)/shard_map/step/pallas_call | solution.py:667
  130.8 4.3 %adam.1 = (f32[32,1152]{1,0:T(8,128)}, f32[32,2304]{1,0:T(8,128)}, f32[32,2304]{1,0:T(8,128)}, f32[32,1152]{1,0:T(8,128)}, f32[2,32,1152]{2,1,0:T(8,128)}, /*ind...) custom-call(f32[2,8,128]{2,1,0:T(8,128)} %get-tuple-element.23.stat, ...), custom_call_target="tpu_custom_call" | custom-call | tf_op jit(solution)/shard_map/adam/pallas_call | solution.py:680

commit v4 on v3

--- a/solution.py
+++ b/solution.py
@@ -574,6 +574,8 @@
         return carry
 
     lax.fori_loop(1, TP, over_tensor, 0, unroll=True)
+    for ref, sem, spot_of in sent:
+        wait_for(ref, sem, spot_of)
     wait_for(sc_buf.at[0, pl.ds(0, TP - 1)], sc_recv, (0,))
     sc_buf[1, me_dp] = jnp.sum(sc_buf[0], axis=0)
 
@@ -586,8 +588,6 @@
     wait_for(sc_buf.at[1, pl.ds(0, DP - 1)], sc_recv, (1,))
     stat[...] = jnp.sum(sc_buf[1], axis=0)
 
-    for ref, sem, spot_of in sent:
-        wait_for(ref, sem, spot_of)
     for k in range(2):
         wait_for(sc_buf.at[k, pl.ds(0, TP - 1)], sc_send, (k,))
 

time: 135 us -> 135 us (level)
  no operation moved by 1% of the time
where the time goes in v4:
time: 135 us
  Pallas kernels  134 us (99%)
    pallas_call x1, Pallas kernels, shards(): pl.pallas_call(body, name='step', out_shape=[jax.ShapeDtypeStruct((ROWS,...  130 us
    pallas_call x1, Pallas kernels, shards(): pl.pallas_call(adam_body, name='adam', out_shape=[jax.ShapeDtypeStruct((R...  4.26 us

profile of v4, /device:TPU:1, one launch (start us, length us, event | category | flops | bytes accessed | tf_op | source)
XLA Modules:
  0.0 135.0 jit_solution(6843960409935271116)
XLA Ops:
  0.6 129.9 %step.1 = (f32[32,1152]{1,0:T(8,128)}, f32[32,2304]{1,0:T(8,128)}, f32[32,2304]{1,0:T(8,128)}, f32[32,1152]{1,0:T(8,128)}, f32[2,8,128]{2,1,0:T(8,128)}) custom-call(bf16[384,1152]{1,0:T(8,128)(2,1)} %tokens.1, bf16[384,1152]{1,0:T(8,128)(2,1)} %target.1, f32[32,1152]{1,0:T(8,128)} %p_pi.1, f32[32,2304]{1,0:T(8,128)} %p_po.1, f32[32,2304]{1,0:T(8,128)} %p_qi.1, ...), custom_call_target="tpu_custom_call" | custom-call | tf_op jit(solution)/shard_map/step/pallas_call | solution.py:667
  130.5 4.3 %adam.1 = (f32[32,1152]{1,0:T(8,128)}, f32[32,2304]{1,0:T(8,128)}, f32[32,2304]{1,0:T(8,128)}, f32[32,1152]{1,0:T(8,128)}, f32[2,32,1152]{2,1,0:T(8,128)}, /*ind...) custom-call(f32[2,8,128]{2,1,0:T(8,128)} %get-tuple-element.23.stat, ...), custom_call_target="tpu_custom_call" | custom-call | tf_op jit(solution)/shard_map/adam/pallas_call | solution.py:680
